TPU v7x, 32 devices: a whole 2x2x4 slice. The times are simulated.
32 devices in a mesh: groups: 2 (over y), blk: 4 (over z), sub: 2 (over x), rep: 2 (over core).
Axes of the slice: x: 2, y: 2, z: 4, core: 2. Of those that a mesh axis runs over, the one named last changes fastest.
Arguments:
- male_features: bfloat16 [32, 65536], P(None, ('groups', 'blk')), parts along dimension 1, may hold values from -4 to 4
- female_features: bfloat16 [32, 65536], P(None, ('groups', 'blk')), parts along dimension 1, may hold values from -4 to 4
- male_mass: float32 [65536], P(('groups', 'blk')), parts along dimension 0, may hold values from 1 to 30
- female_mass: float32 [65536], P(('groups', 'blk')), parts along dimension 0, may hold values from 1 to 30
- base_interaction: float32 [32, 32], replicated, may hold values from -0.1875 to 0.1875
- reform_interaction: float32 [32, 32], replicated, may hold values from -0.1875 to 0.1875
- female_home: int32 [64], P('groups'), parts along dimension 0, may hold values from 0 to 31, as said below
- pair_female: int32 [256], P(('groups', 'blk', 'sub', 'rep')), parts along dimension 0, may hold values from 0 to 31, as said below
- pair_live: int32 [256], P(('groups', 'blk', 'sub', 'rep')), parts along dimension 0, may hold values from 0 to 1, as said below
Outputs:
- male_root: float32 [65536], P(('groups', 'blk')), parts along dimension 0
- female_root: float32 [65536], P(('groups', 'blk')), parts along dimension 0
There are 2 independent parts, one for each index of `groups`. A program takes and returns all parts, laid end to end along the dimension named above; an argument that names none is the same for every part. Nothing has to cross between parts.
Inputs may be any that keep to these rules, and one draw needn't show every extreme that they name: A permutation: female block i is stored as block female_home[i] of the female arrays. `pair_female`: the 8 slots of one device (slots in order of blk, sub, rep) name each male block of its index of blk once; the 4 slots of one male block name distinct female blocks. Among one device's slots at most 2 name female blocks with the same owner (stored block // 8), and on every device some owner is named 2 times. `pair_live`: every male block has a live slot; at each index of blk one device has all its slots live.
All inputs are finite; a program needn't handle non-finite values.
Results may differ from a plain program's by a relative error of at most 0.0003.
Values may be sent and summed in bfloat16 or wider, within the bound.
A program may use at most 128 MiB of HBM per device.

v0:
```python
import math

import jax
import jax.numpy as jnp
from jax import lax
from jax.sharding import PartitionSpec as P

ITERS = 2


rows_per_step = 512


def tile_rows(proj_block, fem_block, row_start, height):
    part_rows = lax.slice_in_dim(proj_block, row_start, row_start + height, axis=1)
    scores = lax.dot_general(
        part_rows,
        fem_block.astype(jnp.float32),
        (((0,), (0,)), ((), ())),
        precision=lax.Precision.HIGHEST,
        preferred_element_type=jnp.float32,
    )
    return jnp.exp(0.5 * scores - math.log(fem_block.shape[1])).astype(jnp.bfloat16)


def row_partial(proj_block, fem_block, female_vals):
    span_cols = proj_block.shape[1]
    height = min(span_cols, rows_per_step)
    pieces = []
    for row_start in range(0, span_cols, height):
        kernel = tile_rows(proj_block, fem_block, row_start, height)
        pieces.append(jnp.dot(kernel, female_vals, preferred_element_type=jnp.float32))
    return jnp.concatenate(pieces)


def column_partial(proj_block, fem_block, male_vals):
    span_cols = proj_block.shape[1]
    height = min(span_cols, rows_per_step)
    column_sum = jnp.zeros((fem_block.shape[1],), jnp.float32)
    for row_start in range(0, span_cols, height):
        kernel = tile_rows(proj_block, fem_block, row_start, height)
        column_sum = column_sum + jnp.dot(
            male_vals[row_start : row_start + height], kernel, preferred_element_type=jnp.float32
        )
    return column_sum


def solve_pot(totals, masses):
    return 2.0 * masses / (totals + jnp.sqrt(totals * totals + 4.0 * masses))


def select_columns(shard_piece, stored, block_size):
    span_cols = shard_piece.shape[-1]
    col_index = stored[:, None] * block_size + jnp.arange(block_size, dtype=jnp.int32)[None, :]
    inside = (col_index >= 0) & (col_index < span_cols)
    selected = jnp.take(shard_piece, jnp.clip(col_index, 0, span_cols - 1), axis=-1)
    selected = jnp.moveaxis(selected, -2, 0)
    keep_mask = inside.reshape((inside.shape[0],) + (1,) * (selected.ndim - 2) + (inside.shape[1],))
    return jnp.where(keep_mask, selected, jnp.zeros_like(selected))


def body(
    male_features,
    female_features,
    male_mass,
    female_mass,
    base_interaction,
    reform_interaction,
    female_home,
    pair_female,
    pair_live,
):
    feat_dim, male_cols = male_features.shape
    blocks_male = pair_female.shape[0]
    block_size = male_cols // blocks_male
    blocks_female = female_features.shape[1] // block_size
    owners = lax.axis_size("blk")
    capacity = (blocks_male + owners - 1) // owners
    all_blocks = female_home.shape[0]
    block_ids = jnp.arange(all_blocks, dtype=jnp.int32)
    stored = jnp.sum(
        jnp.where(pair_female[:, None] == block_ids[None, :], female_home[None, :], 0), axis=1
    )
    owner_of = stored // blocks_female
    local_of = stored % blocks_female
    slot_ids = jnp.arange(blocks_male, dtype=jnp.int32)
    same_owner = (owner_of[:, None] == owner_of[None, :]) & (slot_ids[None, :] < slot_ids[:, None])
    rank_of = jnp.sum(same_owner.astype(jnp.int32), axis=1)
    placed = (owner_of[:, None] == jnp.arange(owners, dtype=jnp.int32)[None, :])[:, :, None] & (
        rank_of[:, None] == jnp.arange(capacity, dtype=jnp.int32)[None, :]
    )[:, None, :]
    placed_real = placed.astype(jnp.float32)
    wanted = jnp.sum(jnp.where(placed, local_of[:, None, None], 0), axis=0)
    asked_for = lax.all_to_all(wanted, "blk", split_axis=0, concat_axis=0, tiled=True)
    asked_hot = (
        asked_for[:, :, None] == jnp.arange(blocks_female, dtype=jnp.int32)[None, None, :]
    ).astype(jnp.float32)
    live_mask = pair_live.astype(jnp.float32)
    coupling = base_interaction + reform_interaction
    projected = jnp.dot(
        coupling.T,
        male_features.astype(jnp.float32),
        precision=lax.Precision.HIGHEST,
        preferred_element_type=jnp.float32,
    )
    proj_blocks = projected.reshape(feat_dim, blocks_male, block_size).transpose(1, 0, 2)
    fem_blocks = select_columns(
        lax.all_gather(female_features, "blk", axis=1, tiled=True), stored, block_size
    )

    def row_slot(slot_item):
        return row_partial(slot_item[0], slot_item[1], slot_item[2])

    def column_slot(slot_item):
        return column_partial(slot_item[0], slot_item[1], slot_item[2])

    female_pot = jnp.sqrt(female_mass)
    male_pot = jnp.zeros_like(male_mass)
    for sweep_index in range(ITERS):
        female_flat = female_pot.astype(jnp.bfloat16)
        female_vals = select_columns(
            lax.all_gather(female_flat, "blk", axis=0, tiled=True), stored, block_size
        )
        row_local = lax.map(row_slot, (proj_blocks, fem_blocks, female_vals)) * live_mask[:, None]
        totals = lax.psum(row_local.reshape(-1), ("sub", "rep"))
        male_pot = solve_pot(totals, male_mass)
        male_vals = male_pot.astype(jnp.bfloat16).reshape(blocks_male, block_size)
        col_local = lax.map(column_slot, (proj_blocks, fem_blocks, male_vals)) * live_mask[:, None]
        outbound = jnp.einsum(
            "mrc,mt->rct", placed_real, col_local, precision=lax.Precision.HIGHEST
        )
        inbound = lax.all_to_all(outbound, "blk", split_axis=0, concat_axis=0, tiled=True)
        gathered_cols = jnp.einsum(
            "rcb,rct->bt", asked_hot, inbound, precision=lax.Precision.HIGHEST
        )
        col_total = lax.psum(gathered_cols.reshape(-1), ("sub", "rep"))
        female_pot = solve_pot(col_total, female_mass)
    male_root = male_pot / jnp.sqrt(male_mass)
    female_root = female_pot / jnp.sqrt(female_mass)
    return (male_root, female_root)


def solution(mesh):
    in_specs = (
        P(None, ("groups", "blk")),
        P(None, ("groups", "blk")),
        P(("groups", "blk")),
        P(("groups", "blk")),
        P(),
        P(),
        P("groups"),
        P(("groups", "blk", "sub", "rep")),
        P(("groups", "blk", "sub", "rep")),
    )
    out_specs = (P(("groups", "blk")), P(("groups", "blk")))
    return jax.shard_map(body, mesh=mesh, in_specs=in_specs, out_specs=out_specs, check_vma=False)
```

profile of v0, /device:TPU:0, one launch (start us, length us, event | category | flops | bytes accessed | tf_op | source)
XLA Modules:
  0.0 438.5 jit_solution(16126791735860608382)
XLA Ops:
  7.3 2.7 copy.27
  11.2 6.3 %all-to-all-start = ((s32[4,1,2]{2,1,0:T(1,128)}), s32[4,1,2]{2,1,0:T(1,128)S(1)}, u32[]{:S(2)}, u32[]{:S(2)}) async-start(s32[4,1,2]{2,1,0:T(1,128)} %copy.29), calls=%async_computation | async-start | bytes 4096 | tf_op jit(solution)/shard_map/all_to_all | solution.py:94
  17.6 14.0 %all_gather.10 = bf16[32768]{0:T(1024)(128)(2,1)S(1)} all-gather(bf16[8192]{0:T(1024)(128)(2,1)S(1)} %sqrt_convert_fusion), channel_id=1, replica_groups=mesh['groups'=2,'blk'=4,'sub'=2,'rep'=2] {'blk'}, dimensions={0}, use_global_device_ids=true | all-gather | bytes 81920 | tf_op jit(solution)/shard_map/all_gather | solution.py:122
  31.7 50.7 %gather_fusion.1 = bf16[8192]{0:T(1024)(128)(2,1)S(1)} fusion(bf16[32768]{0:T(1024)(128)(2,1)S(1)} %all_gather.10, s32[8192]{0:T(1024)S(1)} %bitcast_clamp_fusion), kind=kCustom, calls=%fused_computation.clone | custom fusion | bytes 65536 | tf_op jit(solution)/shard_map/jit(_take)/gather | solution.py:56
  83.6 79.3 %all-gather.2.cloned.1.call-done = bf16[32,32768]{0,1:T(8,128)(2,1)} async-done(((bf16[32,8192]{0,1:T(8,128)(2,1)}), bf16[32,32768]{0,1:T(8,128)(2,1)}) %all-gather.2.cloned.1.call-update) | async-done | bytes 2097168 | tf_op jit(solution)/shard_map/all_gather | solution.py:108
  162.9 32.4 %gather_fusion = bf16[8192,32]{1,0:T(8,128)(2,1)} fusion(bf16[32,32768]{0,1:T(8,128)(2,1)} %all-gather.2.cloned.1.call-done, s32[8192]{0:T(1024)S(1)} %bitcast_clamp_fusion.1), kind=kCustom, calls=%fused_computation.2 | custom fusion | bytes 1081344 | tf_op jit(solution)/shard_map/jit(_take)/gather | solution.py:56
  195.3 1.9 copy.28
  197.3 27.9 %while.52 = (s32[]{:T(128)}, f32[8,1024]{1,0:T(8,128)S(1)}, f32[8,32,1024]{2,1,0:T(8,128)S(1)}, bf16[8,32,1024]{2,1,0:T(8,128)(2,1)S(1)}, bf16[8,1024]{1,0:T(8,128)(2,1)S(1)}, /*index=5*/s32[]{:T(128)}, s32[]{:T(128)}) while((s32[]{:T(128)}, f32[8,1024]{1,0:T(8,128)S(1)}, f32[8,32,1024]{2,1,0:T(8,128)S(1)}, ...), condition=%wide.region_4.6_spmd, body=%wide.region_3.5_spmd.sunk | while | flops 407897088 | bytes 4747365 | solution.py:124
  197.3 1.3 exponential_convert_fusion.16
  200.8 1.3 exponential_convert_fusion.16
  204.3 1.3 exponential_convert_fusion.16
  207.8 1.3 exponential_convert_fusion.16
  214.8 1.3 exponential_convert_fusion.16
  218.3 1.3 exponential_convert_fusion.16
  221.7 1.3 exponential_convert_fusion.16
  225.3 11.3 %psum.28 = f32[8192]{0:T(1024)S(1)} all-reduce(f32[8192]{0:T(1024)S(1)} %bitcast.215), channel_id=1, replica_groups=mesh['groups'=2,'blk'=4,'sub'=2,'rep'=2] {'sub','rep'}, use_global_device_ids=true, to_apply=%region_5.7 | all-reduce | flops 8192 | bytes 65536 | tf_op jit(solution)/shard_map/psum | solution.py:125
  236.7 25.9 %while.53 = (s32[]{:T(128)}, f32[8,1024]{1,0:T(8,128)S(1)}, bf16[8,1024]{1,0:T(8,128)(2,1)S(1)}, f32[8,32,1024]{2,1,0:T(8,128)S(1)}, bf16[8,32,1024]{2,1,0:T(8,128)(2,1)S(1)}, /*index=5*/s32[]{:T(128)}, s32[]{:T(128)}, s32[]{}) while((s32[]{:T(128)}, f32[8,1024]{1,0:T(8,128)S(1)}, bf16[8,1024]{1,0:T(8,128)(2,1)S(1)}, ...), condition=%wide.region_7.9_spmd, body=%wide.region_6.8_spmd.sunk | while | flops 407897088 | bytes 4751485 | solution.py:128
  263.4 3.3 all-to-all-start.1
  266.8 5.5 %all-to-all-done.1 = f32[4,2,1024]{2,1,0:T(2,128)S(1)} async-done(((f32[4,2,1024]{2,1,0:T(2,128)}), f32[4,2,1024]{2,1,0:T(2,128)S(1)}, u32[]{:S(2)}, u32[]{:S(2)}) %all-to-all-start.1) | async-done | bytes 32800 | tf_op jit(solution)/shard_map/all_to_all | solution.py:132
  272.6 10.4 %psum.29 = f32[8192]{0:T(1024)S(1)} all-reduce(f32[8192]{0:T(1024)S(1)} %bitcast.216), channel_id=1, replica_groups=mesh['groups'=2,'blk'=4,'sub'=2,'rep'=2] {'sub','rep'}, use_global_device_ids=true, to_apply=%region_8.10 | all-reduce | flops 8192 | bytes 65536 | tf_op jit(solution)/shard_map/psum | solution.py:136
  283.1 13.4 %all_gather.11 = bf16[32768]{0:T(1024)(128)(2,1)S(1)} all-gather(bf16[8192]{0:T(1024)(128)(2,1)S(1)} %divide_convert_fusion), channel_id=1, replica_groups=mesh['groups'=2,'blk'=4,'sub'=2,'rep'=2] {'blk'}, dimensions={0}, use_global_device_ids=true | all-gather | bytes 81920 | tf_op jit(solution)/shard_map/all_gather | solution.py:122
  296.6 50.7 %gather_fusion.2 = bf16[8192]{0:T(1024)(128)(2,1)S(1)} fusion(bf16[32768]{0:T(1024)(128)(2,1)S(1)} %all_gather.11, s32[8192]{0:T(1024)S(1)} %bitcast_clamp_fusion), kind=kCustom, calls=%fused_computation.1.clone | custom fusion | bytes 65536 | tf_op jit(solution)/shard_map/jit(_take)/gather | solution.py:56
  347.4 27.9 %while.54 = (s32[]{:T(128)}, f32[8,1024]{1,0:T(8,128)S(1)}, f32[8,32,1024]{2,1,0:T(8,128)S(1)}, bf16[8,32,1024]{2,1,0:T(8,128)(2,1)S(1)}, bf16[8,1024]{1,0:T(8,128)(2,1)S(1)}, /*index=5*/s32[]{:T(128)}, s32[]{:T(128)}) while((s32[]{:T(128)}, f32[8,1024]{1,0:T(8,128)S(1)}, f32[8,32,1024]{2,1,0:T(8,128)S(1)}, ...), condition=%wide.region_10.12_spmd, body=%wide.region_9.11_spmd.sunk | while | flops 407897088 | bytes 4747365 | solution.py:124
  349.1 1.3 exponential_convert_fusion.21
  354.4 1.3 exponential_convert_fusion.20
  364.8 1.3 exponential_convert_fusion.20
  368.3 1.3 exponential_convert_fusion.20
  371.8 1.3 exponential_convert_fusion.20
  375.4 10.3 %psum.30 = f32[8192]{0:T(1024)S(1)} all-reduce(f32[8192]{0:T(1024)S(1)} %bitcast.217), channel_id=1, replica_groups=mesh['groups'=2,'blk'=4,'sub'=2,'rep'=2] {'sub','rep'}, use_global_device_ids=true, to_apply=%region_11.13 | all-reduce | flops 8192 | bytes 65536 | tf_op jit(solution)/shard_map/psum | solution.py:125
  386.3 25.9 %while.55 = (s32[]{:T(128)}, f32[8,1024]{1,0:T(8,128)S(1)}, bf16[8,1024]{1,0:T(8,128)(2,1)S(1)}, f32[8,32,1024]{2,1,0:T(8,128)S(1)}, bf16[8,32,1024]{2,1,0:T(8,128)(2,1)S(1)}, /*index=5*/s32[]{:T(128)}, s32[]{:T(128)}, s32[]{}) while((s32[]{:T(128)}, f32[8,1024]{1,0:T(8,128)S(1)}, bf16[8,1024]{1,0:T(8,128)(2,1)S(1)}, ...), condition=%wide.region_13.15_spmd, body=%wide.region_12.14_spmd.sunk | while | flops 407897088 | bytes 4751485 | solution.py:128
  412.4 8.0 %all_to_all.19 = f32[4,2,1024]{2,1,0:T(2,128)S(1)} all-to-all(f32[4,2,1024]{2,1,0:T(2,128)S(1)} %fusion.55), channel_id=1, replica_groups=mesh['groups'=2,'blk'=4,'sub'=2,'rep'=2] {'blk'}, dimensions={0} | all-to-all | bytes 65536 | tf_op jit(solution)/shard_map/all_to_all | solution.py:132
  420.7 10.3 %psum.31 = f32[8192]{0:T(1024)S(1)} all-reduce(f32[8192]{0:T(1024)S(1)} %bitcast.218), channel_id=1, replica_groups=mesh['groups'=2,'blk'=4,'sub'=2,'rep'=2] {'sub','rep'}, use_global_device_ids=true, to_apply=%region_14.16 | all-reduce | flops 8192 | bytes 65536 | tf_op jit(solution)/shard_map/psum | solution.py:136
  (274 shorter events, 96.5 us)
Async XLA Ops:
  7.2 75.3 %copy-start = (bf16[32,8192]{1,0:T(8,128)(2,1)S(1)}, bf16[32,8192]{1,0:T(8,128)(2,1)}, u32[]{:S(2)}) copy-start(bf16[32,8192]{1,0:T(8,128)(2,1)} %param.19) | copy-start | bytes 1572868
  7.2 2.8 copy-start.5
  7.2 2.8 copy-start.6
  7.2 10.4 %copy-start.1 = (f32[8192]{0:T(1024)S(1)}, f32[8192]{0:T(1024)}, u32[]{:S(2)}) copy-start(f32[8192]{0:T(1024)} %param.22) | copy-start | bytes 98308
  7.2 155.7 %all-gather.2.cloned.1.call-start = ((), (), s32[]{:S(2)}) async-start(), calls=%async_computation.3 | async-start | bytes 10485760 | tf_op jit(solution)/shard_map/all_gather | solution.py:108
  11.2 252.2 %all-to-all-start = ((s32[4,1,2]{2,1,0:T(1,128)}), s32[4,1,2]{2,1,0:T(1,128)S(1)}, u32[]{:S(2)}, u32[]{:S(2)}) async-start(s32[4,1,2]{2,1,0:T(1,128)} %copy.29), calls=%async_computation | async-start | bytes 4096 | tf_op jit(solution)/shard_map/all_to_all | solution.py:94
  31.7 50.8 %copy-start.3 = (f32[32,32]{1,0:T(8,128)S(1)}, f32[32,32]{1,0:T(8,128)}, u32[]{:S(2)}) copy-start(f32[32,32]{1,0:T(8,128)} %param.23) | copy-start | bytes 12292
  31.7 50.8 %copy-start.4 = (f32[32,32]{1,0:T(8,128)S(1)}, f32[32,32]{1,0:T(8,128)}, u32[]{:S(2)}) copy-start(f32[32,32]{1,0:T(8,128)} %param.24) | copy-start | bytes 12292
  82.5 0.8 copy-start.7
  197.3 39.3 %copy-start.2 = (f32[8192]{0:T(1024)S(1)}, f32[8192]{0:T(1024)}, u32[]{:S(2)}) copy-start(f32[8192]{0:T(1024)} %param.21) | copy-start | bytes 98308
  263.4 8.9 %all-to-all-start.1 = ((f32[4,2,1024]{2,1,0:T(2,128)}), f32[4,2,1024]{2,1,0:T(2,128)S(1)}, u32[]{:S(2)}, u32[]{:S(2)}) async-start(f32[4,2,1024]{2,1,0:T(2,128)} %fusion.57), calls=%async_computation.1 | async-start | bytes 65536 | tf_op jit(solution)/shard_map/all_to_all | solution.py:132
Sparse Core Ops, SparseCore 0:
  10.1 152.7 all-gather.1
where the time goes:
time: 439 us; the launch traced here: 438 us
  local copies, waits for them, and re-layouts  143 us (33%)
  matrix products  104 us (24%)
  waiting for transfers between devices  84.9 us (19%)
  blocking collectives  77.8 us (18%)
  between operations  14.4 us (3%)
  starting transfers between devices  9.62 us (2%)
    gather x6, local copies, waits for them, and re-layouts, select_columns(): jnp.take(shard_piece, jnp.clip(col_index, 0, span_cols - 1), axis=-1)  136 us
    dot_general x64, matrix products, tile_rows(): lax.dot_general(part_rows, fem_block.astype(jnp.float32), (((0,), (0,)),...  81.6 us
    all_gather x1, waiting for transfers between devices, body(): lax.all_gather(female_features, 'blk', axis=1, tiled=True)  79.3 us
    all_gather x2, blocking collectives, body(): lax.all_gather(female_flat, 'blk', axis=0, tiled=True)  27.5 us
    psum x2, blocking collectives, body(): totals = lax.psum(row_local.reshape(-1), ('sub', 'rep'))  21.6 us
    psum x2, blocking collectives, body(): col_total = lax.psum(gathered_cols.reshape(-1), ('sub', 'rep'))  20.7 us
    dot_general x32, matrix products, row_partial(): jnp.dot(kernel, female_vals, preferred_element_type=jnp.float32)  12 us
  transfers between devices with their start and end apart: 3, of which 2 were waited for; matrix products, arithmetic and copies ran while one was open for 32% of the time, Pallas kernels for 0%

commit v1 on v0

v1 whole, which is shorter than its diff:
```python
import functools
import math

import jax
import jax.numpy as jnp
from jax import lax
from jax.experimental import pallas as pl
from jax.experimental.pallas import tpu as pltpu
from jax.sharding import PartitionSpec as P

ITERS = 2
MESH = pl.DeviceIdType.MESH


def solve_pot(totals, masses):
    return 2.0 * masses / (totals + jnp.sqrt(totals * totals + 4.0 * masses))


def sweeps(
    sizes,
    male_ref,
    fem_ref,
    mmass_ref,
    fmass_ref,
    base_ref,
    reform_ref,
    pick_ref,
    live_ref,
    mroot_ref,
    froot_ref,
    kern,
    vals,
    lines,
    rows,
    row_in,
    row_out,
    cols,
    col_out,
    col_in,
    vals_out,
    vals_in,
    last_out,
    last_in,
    row_send,
    row_recv,
    col_send,
    col_recv,
    val_send,
    val_recv,
    last_send,
    last_recv,
):
    owners, n_sub, n_rep = sizes
    mates = n_sub * n_rep
    peers = owners * mates
    slots, block = mmass_ref.shape
    stored_blocks = fmass_ref.shape[0]
    feat = male_ref.shape[0]
    width = col_out.shape[-1]
    chunks = block // width
    group = lax.axis_index("groups")
    my_blk = lax.axis_index("blk")
    my_mate = lax.axis_index("sub") * n_rep + lax.axis_index("rep")
    me = my_blk * mates + my_mate

    def place(peer):
        blk = lax.div(peer, mates)
        mate = lax.rem(peer, mates)
        return (group, blk, lax.div(mate, n_rep), lax.rem(mate, n_rep))

    def mate_place(mate):
        return (group, my_blk, lax.div(mate, n_rep), lax.rem(mate, n_rep))

    def wait_all(ref, sem):
        pltpu.make_async_copy(ref, ref, sem).wait()

    barrier = pltpu.get_barrier_semaphore()

    @pl.loop(1, peers)
    def _(step):
        pl.semaphore_signal(
            barrier, inc=1, device_id=place(lax.rem(me + step, peers)), device_id_type=MESH
        )

    pl.semaphore_wait(barrier, peers - 1)

    def to_peers(src_of, dst, send_sem, recv_sem):
        @pl.loop(1, peers)
        def _(step):
            peer = lax.rem(me + step, peers)
            pltpu.make_async_remote_copy(
                src_ref=src_of(peer),
                dst_ref=dst.at[step],
                send_sem=send_sem,
                recv_sem=recv_sem,
                device_id=place(peer),
                device_id_type=MESH,
            ).start()

    def to_mates(src, dst, send_sem, recv_sem):
        @pl.loop(1, mates)
        def _(step):
            pltpu.make_async_remote_copy(
                src_ref=src,
                dst_ref=dst.at[step],
                send_sem=send_sem,
                recv_sem=recv_sem,
                device_id=mate_place(lax.rem(my_mate + step, mates)),
                device_id_type=MESH,
            ).start()

    def my_chunk(ref):
        start = pl.multiple_of(lax.rem(my_mate, chunks) * width, width)
        return ref[:, pl.ds(start, width)]

    def select_vals(turn):
        for owner in range(owners):
            for chunk in range(chunks):
                index = lax.rem(me - (owner * mates + chunk) + peers, peers)
                vals[
                    owner * stored_blocks : (owner + 1) * stored_blocks,
                    chunk * width : (chunk + 1) * width,
                ] = vals_in[turn, index]
        lines[...] = jnp.dot(
            pick_ref[...].astype(jnp.bfloat16),
            vals[...].astype(jnp.bfloat16),
            preferred_element_type=jnp.float32,
        )

    def line_of(slot):
        return jnp.broadcast_to(lines[pl.ds(slot, 1), :], (16, block)).astype(jnp.bfloat16)

    fmass_mine = my_chunk(fmass_ref)
    first = jnp.sqrt(fmass_mine)
    vals_out[0] = first
    vals_in[0, 0] = first
    to_peers(lambda peer: vals_out.at[0], vals_in.at[0], val_send.at[0], val_recv.at[0])
    wait_all(vals_in.at[0, pl.ds(1, peers - 1)], val_recv.at[0])
    select_vals(0)

    coupling = (base_ref[...] + reform_ref[...]) * (0.5 / math.log(2.0))
    shift = math.log2(block) / 16

    for sweep in range(ITERS):

        @pl.loop(0, slots)
        def _(slot):
            line = line_of(slot)
            if sweep == 0:
                fem = fem_ref[slot]
                men = male_ref[:, pl.ds(pl.multiple_of(slot * block, block), block)]
                projected = lax.dot_general(
                    coupling,
                    men.astype(jnp.float32),
                    (((0,), (0,)), ((), ())),
                    precision=lax.Precision.HIGHEST,
                    preferred_element_type=jnp.float32,
                )
                high = projected.astype(jnp.bfloat16).astype(jnp.float32)
                rest = projected - high
                middle = rest.astype(jnp.bfloat16).astype(jnp.float32)
                left = jnp.concatenate(
                    [high, middle, rest - middle, jnp.full((16, block), -shift, jnp.float32)], axis=0
                )
                left = left.T.astype(jnp.bfloat16)
                right = jnp.concatenate(
                    [fem, fem, fem, jnp.ones((16, block), jnp.bfloat16)], axis=0
                )
                height = block // 4
                for part in range(4):
                    span = slice(part * height, (part + 1) * height)
                    scores = jnp.dot(left[span], right, preferred_element_type=jnp.float32)
                    tile = jnp.exp2(scores).astype(jnp.bfloat16)
                    kern[slot, span, :] = tile
                    total = lax.dot_general(
                        line,
                        tile,
                        (((1,), (1,)), ((), ())),
                        preferred_element_type=jnp.float32,
                    )
                    rows[pl.ds(slot, 1), span] = total[0:1]
            else:
                total = lax.dot_general(
                    line,
                    kern[slot],
                    (((1,), (1,)), ((), ())),
                    preferred_element_type=jnp.float32,
                )
                rows[pl.ds(slot, 1), :] = total[0:1]

        partial = rows[...] * live_ref[...]
        row_out[sweep] = partial
        row_in[sweep, 0] = partial
        to_mates(row_out.at[sweep], row_in.at[sweep], row_send.at[sweep], row_recv.at[sweep])
        wait_all(row_in.at[sweep, pl.ds(1, mates - 1)], row_recv.at[sweep])
        totals = row_in[sweep, lax.rem(my_mate + mates, mates)]
        for mate in range(1, mates):
            totals = totals + row_in[sweep, lax.rem(my_mate - mate + mates, mates)]
        male_pot = solve_pot(totals, mmass_ref[...])
        lines[...] = male_pot
        if sweep == ITERS - 1:
            mroot_ref[...] = male_pot / jnp.sqrt(mmass_ref[...])

        @pl.loop(0, slots)
        def _(slot):
            total = jnp.dot(line_of(slot), kern[slot], preferred_element_type=jnp.float32)
            cols[pl.ds(slot, 1), :] = total[0:1]

        dense = lax.dot_general(
            pick_ref[...] * live_ref[...],
            cols[...],
            (((0,), (0,)), ((), ())),
            precision=lax.Precision.HIGHEST,
            preferred_element_type=jnp.float32,
        )
        for owner in range(owners):
            for mate in range(mates):
                begin = (mate % chunks) * width
                col_out[sweep, owner * mates + mate] = dense[
                    owner * stored_blocks : (owner + 1) * stored_blocks, begin : begin + width
                ]

        col_in[sweep, 0] = col_out[sweep, me]
        to_peers(
            lambda peer: col_out.at[sweep, peer],
            col_in.at[sweep],
            col_send.at[sweep],
            col_recv.at[sweep],
        )
        wait_all(col_in.at[sweep, pl.ds(1, peers - 1)], col_recv.at[sweep])
        col_total = lax.fori_loop(
            1, peers, lambda step, total: total + col_in[sweep, step], col_in[sweep, 0]
        )
        female_pot = solve_pot(col_total, fmass_mine)
        if sweep < ITERS - 1:
            turn = sweep + 1
            vals_out[turn] = female_pot
            vals_in[turn, 0] = female_pot
            to_peers(
                lambda peer: vals_out.at[turn], vals_in.at[turn], val_send.at[turn], val_recv.at[turn]
            )
            wait_all(vals_in.at[turn, pl.ds(1, peers - 1)], val_recv.at[turn])
            select_vals(turn)
        else:
            root = female_pot / jnp.sqrt(fmass_mine)
            last_out[...] = root
            last_in[0] = root
            to_mates(last_out, last_in, last_send, last_recv)
            wait_all(last_in.at[pl.ds(1, mates - 1)], last_recv)
            for chunk in range(chunks):
                froot_ref[:, chunk * width : (chunk + 1) * width] = last_in[
                    lax.rem(my_mate - chunk + mates, mates)
                ]

    for sweep in range(ITERS):
        wait_all(row_in.at[sweep, pl.ds(1, mates - 1)], row_send.at[sweep])
        wait_all(col_in.at[sweep, pl.ds(1, peers - 1)], col_send.at[sweep])
        wait_all(vals_in.at[sweep, pl.ds(1, peers - 1)], val_send.at[sweep])
    wait_all(last_in.at[pl.ds(1, mates - 1)], last_send)


def copy_block(at_ref, from_ref, to_ref):
    to_ref[...] = from_ref[...]


def body(
    male_features,
    female_features,
    male_mass,
    female_mass,
    base_interaction,
    reform_interaction,
    female_home,
    pair_female,
    pair_live,
):
    owners, n_sub, n_rep = (lax.axis_size(name) for name in ("blk", "sub", "rep"))
    mates = n_sub * n_rep
    peers = owners * mates
    slots = pair_female.shape[0]
    block = male_features.shape[1] // slots
    stored_blocks = female_features.shape[1] // block
    width = max(128, block // mates)
    ids = jnp.arange(female_home.shape[0], dtype=jnp.int32)
    stored = jnp.sum(jnp.where(pair_female[:, None] == ids[None, :], female_home[None, :], 0), axis=1)
    pick = (stored[:, None] == ids[None, :]).astype(jnp.float32)
    live = pair_live.astype(jnp.float32)[:, None]
    gathered = lax.all_gather(female_features, "blk")
    wanted = pl.pallas_call(
        copy_block,
        grid_spec=pltpu.PrefetchScalarGridSpec(
            num_scalar_prefetch=1,
            grid=(slots,),
            in_specs=[
                pl.BlockSpec(
                    (1, gathered.shape[1], block),
                    lambda slot, at: (
                        lax.div(at[slot], stored_blocks),
                        0,
                        lax.rem(at[slot], stored_blocks),
                    ),
                )
            ],
            out_specs=pl.BlockSpec((1, gathered.shape[1], block), lambda slot, at: (slot, 0, 0)),
        ),
        out_shape=jax.ShapeDtypeStruct((slots, gathered.shape[1], block), jnp.bfloat16),
        name="wanted_blocks",
    )(stored, gathered)
    vmem = pl.BlockSpec(memory_space=pltpu.VMEM)
    dma = pltpu.SemaphoreType.DMA
    f32 = jnp.float32
    male_root, female_root = pl.pallas_call(
        functools.partial(sweeps, (owners, n_sub, n_rep)),
        out_shape=(
            jax.ShapeDtypeStruct((slots, block), f32),
            jax.ShapeDtypeStruct((stored_blocks, block), f32),
        ),
        in_specs=[vmem] * 8,
        out_specs=(vmem, vmem),
        scratch_shapes=[
            pltpu.VMEM((slots, block, block), jnp.bfloat16),
            pltpu.VMEM((owners * stored_blocks, block), f32),
            pltpu.VMEM((slots, block), f32),
            pltpu.VMEM((slots, block), f32),
            pltpu.VMEM((ITERS, mates, slots, block), f32),
            pltpu.VMEM((ITERS, slots, block), f32),
            pltpu.VMEM((slots, block), f32),
            pltpu.VMEM((ITERS, peers, stored_blocks, width), f32),
            pltpu.VMEM((ITERS, peers, stored_blocks, width), f32),
            pltpu.VMEM((ITERS, stored_blocks, width), f32),
            pltpu.VMEM((ITERS, peers, stored_blocks, width), f32),
            pltpu.VMEM((stored_blocks, width), f32),
            pltpu.VMEM((mates, stored_blocks, width), f32),
            dma((ITERS,)),
            dma((ITERS,)),
            dma((ITERS,)),
            dma((ITERS,)),
            dma((ITERS,)),
            dma((ITERS,)),
            dma,
            dma,
        ],
        compiler_params=pltpu.CompilerParams(
            collective_id=0, has_side_effects=True, vmem_limit_bytes=50 * 2**20
        ),
        name="sweeps",
    )(
        male_features,
        wanted,
        male_mass.reshape(slots, block),
        female_mass.reshape(stored_blocks, block),
        base_interaction,
        reform_interaction,
        pick,
        live,
    )
    return male_root.reshape(-1), female_root.reshape(-1)


def solution(mesh):
    in_specs = (
        P(None, ("groups", "blk")),
        P(None, ("groups", "blk")),
        P(("groups", "blk")),
        P(("groups", "blk")),
        P(),
        P(),
        P("groups"),
        P(("groups", "blk", "sub", "rep")),
        P(("groups", "blk", "sub", "rep")),
    )
    out_specs = (P(("groups", "blk")), P(("groups", "blk")))
    return jax.shard_map(body, mesh=mesh, in_specs=in_specs, out_specs=out_specs, check_vma=False)
```

time: 439 us -> 130 us (0.30)
  local copies, waits for them, and re-layouts: 143 us -> 3.31 us
  matrix products: 104 us -> 0 us
  blocking collectives: 77.8 us -> 0 us
  Pallas kernels: 0 us -> 62.2 us
  waiting for transfers between devices: 84.9 us -> 47.8 us
  starting transfers between devices: 9.62 us -> 0.04 us
    gather x6 -> x0, local copies, waits for them, and re-layouts: 136 us -> none  [select_columns(): jnp.take(shard_piece, jnp.clip(col_index, 0, span_cols - 1), axis=-1)]
    dot_general x133 -> x0, matrix products: 104 us -> none  [the longest x64 81.6 us: tile_rows(): lax.dot_general(part_rows, fem_block.astype(jnp.float32), (((0,), (0,)),...]
    pallas_call x0 -> x2, Pallas kernels: none -> 62.2 us  [the longest x1 56.8 us: body(): pl.pallas_call(functools.partial(sweeps, (owners, n_sub, n_rep)), out_sha...]
    psum x4 -> x0, blocking collectives: 42.3 us -> none  [the longest x2 21.6 us: body(): totals = lax.psum(row_local.reshape(-1), ('sub', 'rep'))]
    all_gather x1, waiting for transfers between devices: 79.3 us -> 47.1 us  [body(): gathered = lax.all_gather(female_features, 'blk')]
    all_gather x2 -> x0, blocking collectives: 27.5 us -> none  [body(): lax.all_gather(female_flat, 'blk', axis=0, tiled=True)]
    all_to_all x2 -> x0, starting transfers between devices: 9.58 us -> none  [the longest x1 6.32 us: body(): lax.all_to_all(wanted, 'blk', split_axis=0, concat_axis=0, tiled=True)]
    all_to_all x1 -> x0, blocking collectives: 8.01 us -> none  [body(): lax.all_to_all(outbound, 'blk', split_axis=0, concat_axis=0, tiled=True)]
  transfers between devices with their start and end apart: 3 -> 1, of which waited for: 2 -> 1; matrix products, arithmetic and copies ran while one was open for 32% -> 2% of each run, Pallas kernels for 0% -> 0%
where the time goes in v1:
time: 130 us; the launch traced here: 129 us
  Pallas kernels  62.2 us (48%)
  waiting for transfers between devices  47.8 us (37%)
  between operations  14.1 us (11%)
  local copies, waits for them, and re-layouts  3.31 us (3%)
  other arithmetic  1.58 us (1%)
    pallas_call x1, Pallas kernels, body(): pl.pallas_call(functools.partial(sweeps, (owners, n_sub, n_rep)), out_sha...  56.8 us
    all_gather x1, waiting for transfers between devices, body(): gathered = lax.all_gather(female_features, 'blk')  47.1 us
    pallas_call x1, Pallas kernels, body(): pl.pallas_call(copy_block, grid_spec=pltpu.PrefetchScalarGridSpec(num_sca...  5.39 us
  transfers between devices with their start and end apart: 1, of which 1 were waited for; matrix products, arithmetic and copies ran while one was open for 2% of the time, Pallas kernels for 0%

profile of v1, /device:TPU:0, one launch (start us, length us, event | category | flops | bytes accessed | tf_op | source)
XLA Modules:
  0.0 129.0 jit_solution(3639335263326764554)
XLA Ops:
  7.2 0.0 copy-start.3
  7.2 0.0 copy-start.2
  7.2 0.0 copy-start.1
  7.2 0.0 all-gather.3.cloned.1.call-start
  7.2 0.7 all-gather.3.cloned.1.call-update
  7.9 0.7 convert_bitcast_fusion
  8.6 0.1 copy.12.live_ref
  8.7 0.8 reshape.19.mmass_ref
  9.4 0.8 reshape.20.fmass_ref
  10.2 0.9 select_reduce_fusion.at_ref
  11.1 0.0 copy-start.4
  11.1 0.1 fusion.pick_ref
  11.1 47.1 %all-gather.3.cloned.1.call-done = bf16[128,8192]{1,0:T(8,128)(2,1)} async-done(((bf16[32,8192]{1,0:T(8,128)(2,1)}), bf16[128,8192]{1,0:T(8,128)(2,1)}) %all-gather.3.cloned.1.call-update) | async-done | bytes 2097168 | tf_op jit(solution)/shard_map/all_gather | solution.py:288
  58.3 0.0 copy-done.4
  58.3 5.4 %wanted_blocks.1.fem_ref = bf16[8,32,1024]{2,1,0:T(8,128)(2,1)} custom-call(s32[8]{0:T(128)} %copy-done.4, bf16[4,32,8192]{2,1,0:T(8,128)(2,1)} %bitcast.11), custom_call_target="tpu_custom_call" | custom-call | tf_op jit(solution)/shard_map/wanted_blocks/pallas_call | solution.py:289
  63.7 0.0 copy-done.3
  63.7 0.0 copy-done.2
  63.7 0.0 copy-done.1
  63.7 0.0 copy-start
  63.7 1.0 copy-done
  64.7 56.8 %sweeps.1 = (f32[8,1024]{1,0:T(8,128)S(1)}, f32[8,1024]{1,0:T(8,128)S(1)}) custom-call(bf16[32,8192]{1,0:T(8,128)(2,1)S(1)} %copy-done.1, bf16[8,32,1024]{2,1,0:T(8,128)(2,1)S(1)} %copy-done, f32[8,1024]{1,0:T(8,128)S(1)} %reshape.19.mmass_ref, f32[8,1024]{1,0:T(8,128)S(1)} %reshape.20.fmass_ref, f32[32,32]{1,0:T(8,128)S(1)} %copy-done.2, ...), custom_call_target="tpu_custom_call" | custom-call | tf_op jit(solution)/shard_map/sweeps/pallas_call | solution.py:312
  121.5 0.6 copy_bitcast_fusion
Async XLA Ops:
  7.2 56.5 %copy-start.3 = (f32[32,32]{1,0:T(8,128)S(1)}, f32[32,32]{1,0:T(8,128)}, u32[]{:S(2)}) copy-start(f32[32,32]{1,0:T(8,128)} %reform_ref.1) | copy-start | bytes 12292
  7.2 56.5 %copy-start.2 = (f32[32,32]{1,0:T(8,128)S(1)}, f32[32,32]{1,0:T(8,128)}, u32[]{:S(2)}) copy-start(f32[32,32]{1,0:T(8,128)} %base_ref.1) | copy-start | bytes 12292
  7.2 56.5 %copy-start.1 = (bf16[32,8192]{1,0:T(8,128)(2,1)S(1)}, bf16[32,8192]{1,0:T(8,128)(2,1)}, u32[]{:S(2)}) copy-start(bf16[32,8192]{1,0:T(8,128)(2,1)} %male_ref.1) | copy-start | bytes 1572868
  7.2 51.1 %all-gather.3.cloned.1.call-start = ((), (), s32[]{:S(2)}) async-start(), calls=%async_computation | async-start | bytes 2621440 | tf_op jit(solution)/shard_map/all_gather | solution.py:288
  11.1 47.2 %copy-start.4 = (s32[8]{0:T(128)}, s32[8]{0:T(128)S(1)}, u32[]{:S(2)}) copy-start(s32[8]{0:T(128)S(1)} %select_reduce_fusion.at_ref) | copy-start | bytes 100
  63.7 1.0 copy-start
Sparse Core Ops, SparseCore 0:
  9.6 48.6 all-gather.2

commit v2 on v1

--- a/solution.py
+++ b/solution.py
@@ -24,14 +24,24 @@
     fmass_ref,
     base_ref,
     reform_ref,
-    pick_ref,
-    live_ref,
+    info_ref,
+    spot_ref,
     mroot_ref,
     froot_ref,
     kern,
+    women,
+    men,
+    ask_out,
+    ask_in,
+    fem_out,
+    fem_in,
+    place,
+    pick,
+    line_t,
+    row_t,
     vals,
     lines,
-    rows,
+    place_t,
     row_in,
     row_out,
     cols,
@@ -49,6 +59,10 @@
     val_recv,
     last_send,
     last_recv,
+    ask_send,
+    ask_recv,
+    fem_send,
+    fem_recv,
 ):
     owners, n_sub, n_rep = sizes
     mates = n_sub * n_rep
@@ -56,6 +70,8 @@
     slots, block = mmass_ref.shape
     stored_blocks = fmass_ref.shape[0]
     feat = male_ref.shape[0]
+    spots = kern.shape[0]
+    depth = spots // owners
     width = col_out.shape[-1]
     chunks = block // width
     group = lax.axis_index("groups")
@@ -63,7 +79,7 @@
     my_mate = lax.axis_index("sub") * n_rep + lax.axis_index("rep")
     me = my_blk * mates + my_mate
 
-    def place(peer):
+    def device_of(peer):
         blk = lax.div(peer, mates)
         mate = lax.rem(peer, mates)
         return (group, blk, lax.div(mate, n_rep), lax.rem(mate, n_rep))
@@ -79,7 +95,7 @@
     @pl.loop(1, peers)
     def _(step):
         pl.semaphore_signal(
-            barrier, inc=1, device_id=place(lax.rem(me + step, peers)), device_id_type=MESH
+            barrier, inc=1, device_id=device_of(lax.rem(me + step, peers)), device_id_type=MESH
         )
 
     pl.semaphore_wait(barrier, peers - 1)
@@ -93,7 +109,7 @@
                 dst_ref=dst.at[step],
                 send_sem=send_sem,
                 recv_sem=recv_sem,
-                device_id=place(peer),
+                device_id=device_of(peer),
                 device_id_type=MESH,
             ).start()
 
@@ -121,11 +137,15 @@
                     owner * stored_blocks : (owner + 1) * stored_blocks,
                     chunk * width : (chunk + 1) * width,
                 ] = vals_in[turn, index]
-        lines[...] = jnp.dot(
-            pick_ref[...].astype(jnp.bfloat16),
+        picked = jnp.dot(
+            pick[...].astype(jnp.bfloat16),
             vals[...].astype(jnp.bfloat16),
             preferred_element_type=jnp.float32,
         )
+        padded = jnp.concatenate(
+            [picked, jnp.zeros((line_t.shape[1] - spots, block), jnp.float32)], axis=0
+        )
+        line_t[...] = padded.T.astype(jnp.bfloat16)
 
     def line_of(slot):
         return jnp.broadcast_to(lines[pl.ds(slot, 1), :], (16, block)).astype(jnp.bfloat16)
@@ -135,23 +155,93 @@
     vals_out[0] = first
     vals_in[0, 0] = first
     to_peers(lambda peer: vals_out.at[0], vals_in.at[0], val_send.at[0], val_recv.at[0])
+    def mix(weights, lines_in):
+        total = weights[:, :1] * lines_in[:1, :]
+        for index in range(1, lines_in.shape[0]):
+            total = total + weights[:, index : index + 1] * lines_in[index : index + 1, :]
+        return total
+
+    def equals(line, count):
+        lane = lax.broadcasted_iota(jnp.int32, (line.shape[0], count), 1).astype(jnp.float32)
+        return jnp.where(line[:, :1] == lane, 1.0, 0.0)
+
+    slot_at, local_at, stored_at, live_at = (spot_ref[index] for index in range(4))
+    place[...] = equals(info_ref[0], spots)
+    place_t[...] = equals(slot_at, slots)
+    pick[...] = equals(stored_at, stored_blocks * owners)
+    for step in range(owners):
+        ask_out[step, :depth] = local_at[step * depth : (step + 1) * depth]
+
+    @pl.loop(1, owners)
+    def _(step):
+        to = lax.rem(my_blk - step + owners, owners) * mates + my_mate
+        pltpu.make_async_remote_copy(
+            src_ref=ask_out.at[step],
+            dst_ref=ask_in.at[step],
+            send_sem=ask_send,
+            recv_sem=ask_recv,
+            device_id=device_of(to),
+            device_id_type=MESH,
+        ).start()
+
+    for index in range(slots):
+        men[index * feat : (index + 1) * feat] = male_ref[:, index * block : (index + 1) * block]
+    for index in range(stored_blocks):
+        women[index * feat : (index + 1) * feat] = fem_ref[:, index * block : (index + 1) * block]
+
+    def choose(line, source):
+        total = source.shape[0]
+        target = jnp.broadcast_to(line[:, :1], (feat, total)) * feat
+        target = target + lax.broadcasted_iota(jnp.int32, (feat, total), 0).astype(jnp.float32)
+        column = lax.broadcasted_iota(jnp.int32, (feat, total), 1).astype(jnp.float32)
+        hot = jnp.where(column == target, 1.0, 0.0).astype(jnp.bfloat16)
+        return jnp.dot(hot, source[...], preferred_element_type=jnp.float32)
+
+    for deep in range(depth):
+        fem_in[deep] = choose(ask_out[0, deep : deep + 1], women).astype(jnp.bfloat16)
+    wait_all(ask_in.at[pl.ds(1, owners - 1)], ask_recv)
+
+    @pl.loop(1, owners)
+    def _(step):
+        for deep in range(depth):
+            fem_out[step * depth + deep] = choose(
+                ask_in[step, deep : deep + 1], women
+            ).astype(jnp.bfloat16)
+        to = lax.rem(my_blk + step, owners) * mates + my_mate
+        pltpu.make_async_remote_copy(
+            src_ref=fem_out.at[pl.ds(step * depth, depth)],
+            dst_ref=fem_in.at[pl.ds(step * depth, depth)],
+            send_sem=fem_send.at[step],
+            recv_sem=fem_recv.at[step],
+            device_id=device_of(to),
+            device_id_type=MESH,
+        ).start()
+
     wait_all(vals_in.at[0, pl.ds(1, peers - 1)], val_recv.at[0])
     select_vals(0)
 
     coupling = (base_ref[...] + reform_ref[...]) * (0.5 / math.log(2.0))
     shift = math.log2(block) / 16
+    column = lax.broadcasted_iota(jnp.int32, (block // 4, line_t.shape[1]), 1)
 
     for sweep in range(ITERS):
 
-        @pl.loop(0, slots)
-        def _(slot):
-            line = line_of(slot)
+        row_t[...] = jnp.zeros_like(row_t)
+
+        @pl.loop(0, spots)
+        def _(spot):
+            height = block // 4
             if sweep == 0:
-                fem = fem_ref[slot]
-                men = male_ref[:, pl.ds(pl.multiple_of(slot * block, block), block)]
+
+                @pl.when(jnp.logical_and(spot >= depth, lax.rem(spot, depth) == 0))
+                def _():
+                    step = lax.div(spot, depth)
+                    wait_all(fem_in.at[pl.ds(spot, depth)], fem_recv.at[step])
+
+                fem = fem_in[spot]
                 projected = lax.dot_general(
                     coupling,
-                    men.astype(jnp.float32),
+                    choose(spot_ref[0, pl.ds(spot, 1), :], men),
                     (((0,), (0,)), ((), ())),
                     precision=lax.Precision.HIGHEST,
                     preferred_element_type=jnp.float32,
@@ -166,29 +256,18 @@
                 right = jnp.concatenate(
                     [fem, fem, fem, jnp.ones((16, block), jnp.bfloat16)], axis=0
                 )
-                height = block // 4
-                for part in range(4):
-                    span = slice(part * height, (part + 1) * height)
+            for part in range(4):
+                span = slice(part * height, (part + 1) * height)
+                if sweep == 0:
                     scores = jnp.dot(left[span], right, preferred_element_type=jnp.float32)
                     tile = jnp.exp2(scores).astype(jnp.bfloat16)
-                    kern[slot, span, :] = tile
-                    total = lax.dot_general(
-                        line,
-                        tile,
-                        (((1,), (1,)), ((), ())),
-                        preferred_element_type=jnp.float32,
-                    )
-                    rows[pl.ds(slot, 1), span] = total[0:1]
-            else:
-                total = lax.dot_general(
-                    line,
-                    kern[slot],
-                    (((1,), (1,)), ((), ())),
-                    preferred_element_type=jnp.float32,
-                )
-                rows[pl.ds(slot, 1), :] = total[0:1]
-
-        partial = rows[...] * live_ref[...]
+                    kern[spot, span, :] = tile
+                else:
+                    tile = kern[spot, span, :]
+                total = jnp.dot(tile, line_t[...], preferred_element_type=jnp.float32)
+                row_t[span, :] = row_t[span, :] + jnp.where(column == spot, total, 0.0)
+
+        partial = mix(place[...], jnp.where(live_at[:, :1] > 0.0, row_t[...].T[:spots], 0.0))
         row_out[sweep] = partial
         row_in[sweep, 0] = partial
         to_mates(row_out.at[sweep], row_in.at[sweep], row_send.at[sweep], row_recv.at[sweep])
@@ -197,18 +276,18 @@
         for mate in range(1, mates):
             totals = totals + row_in[sweep, lax.rem(my_mate - mate + mates, mates)]
         male_pot = solve_pot(totals, mmass_ref[...])
-        lines[...] = male_pot
+        lines[...] = mix(place_t[...], male_pot)
         if sweep == ITERS - 1:
             mroot_ref[...] = male_pot / jnp.sqrt(mmass_ref[...])
 
-        @pl.loop(0, slots)
+        @pl.loop(0, spots)
         def _(slot):
             total = jnp.dot(line_of(slot), kern[slot], preferred_element_type=jnp.float32)
             cols[pl.ds(slot, 1), :] = total[0:1]
 
         dense = lax.dot_general(
-            pick_ref[...] * live_ref[...],
-            cols[...],
+            pick[...],
+            jnp.where(live_at[:, :1] > 0.0, cols[...], 0.0),
             (((0,), (0,)), ((), ())),
             precision=lax.Precision.HIGHEST,
             preferred_element_type=jnp.float32,
@@ -257,10 +336,11 @@
         wait_all(col_in.at[sweep, pl.ds(1, peers - 1)], col_send.at[sweep])
         wait_all(vals_in.at[sweep, pl.ds(1, peers - 1)], val_send.at[sweep])
     wait_all(last_in.at[pl.ds(1, mates - 1)], last_send)
-
-
-def copy_block(at_ref, from_ref, to_ref):
-    to_ref[...] = from_ref[...]
+    wait_all(ask_in.at[pl.ds(1, owners - 1)], ask_send)
+
+    @pl.loop(1, owners)
+    def _(step):
+        wait_all(fem_in.at[pl.ds(step * depth, depth)], fem_send.at[step])
 
 
 def body(
@@ -283,29 +363,20 @@
     width = max(128, block // mates)
     ids = jnp.arange(female_home.shape[0], dtype=jnp.int32)
     stored = jnp.sum(jnp.where(pair_female[:, None] == ids[None, :], female_home[None, :], 0), axis=1)
-    pick = (stored[:, None] == ids[None, :]).astype(jnp.float32)
-    live = pair_live.astype(jnp.float32)[:, None]
-    gathered = lax.all_gather(female_features, "blk")
-    wanted = pl.pallas_call(
-        copy_block,
-        grid_spec=pltpu.PrefetchScalarGridSpec(
-            num_scalar_prefetch=1,
-            grid=(slots,),
-            in_specs=[
-                pl.BlockSpec(
-                    (1, gathered.shape[1], block),
-                    lambda slot, at: (
-                        lax.div(at[slot], stored_blocks),
-                        0,
-                        lax.rem(at[slot], stored_blocks),
-                    ),
-                )
-            ],
-            out_specs=pl.BlockSpec((1, gathered.shape[1], block), lambda slot, at: (slot, 0, 0)),
-        ),
-        out_shape=jax.ShapeDtypeStruct((slots, gathered.shape[1], block), jnp.bfloat16),
-        name="wanted_blocks",
-    )(stored, gathered)
+    spot_depth = -(-slots // owners)
+    spots = owners * spot_depth
+    owner = stored // stored_blocks
+    order = jnp.arange(slots, dtype=jnp.int32)
+    earlier = (owner[:, None] == owner[None, :]) & (order[None, :] < order[:, None])
+    rank = jnp.sum(earlier.astype(jnp.int32), axis=1)
+    step = (lax.axis_index("blk") - owner + owners) % owners
+    spot = step * spot_depth + rank
+    info = jnp.broadcast_to(spot.astype(jnp.float32)[None, :, None], (1, slots, 128))
+    at_spot = spot[None, :, None] == jnp.arange(spots, dtype=jnp.int32)[None, None, :]
+    facts = jnp.stack([order, stored % stored_blocks, stored, pair_live])
+    spot_info = jnp.sum(jnp.where(at_spot, facts[:, :, None], 0), axis=1)
+    spot_info = jnp.broadcast_to(spot_info.astype(jnp.float32)[:, :, None], (4, spots, 128))
+    feat = male_features.shape[0]
     vmem = pl.BlockSpec(memory_space=pltpu.VMEM)
     dma = pltpu.SemaphoreType.DMA
     f32 = jnp.float32
@@ -318,13 +389,23 @@
         in_specs=[vmem] * 8,
         out_specs=(vmem, vmem),
         scratch_shapes=[
-            pltpu.VMEM((slots, block, block), jnp.bfloat16),
+            pltpu.VMEM((spots, block, block), jnp.bfloat16),
+            pltpu.VMEM((stored_blocks * feat, block), jnp.bfloat16),
+            pltpu.VMEM((slots * feat, block), jnp.bfloat16),
+            pltpu.VMEM((owners, 8, 128), f32),
+            pltpu.VMEM((owners, 8, 128), f32),
+            pltpu.VMEM((spots, feat, block), jnp.bfloat16),
+            pltpu.VMEM((spots, feat, block), jnp.bfloat16),
+            pltpu.VMEM((slots, spots), f32),
+            pltpu.VMEM((spots, owners * stored_blocks), f32),
+            pltpu.VMEM((block, 128), jnp.bfloat16),
+            pltpu.VMEM((block, 128), f32),
             pltpu.VMEM((owners * stored_blocks, block), f32),
-            pltpu.VMEM((slots, block), f32),
-            pltpu.VMEM((slots, block), f32),
+            pltpu.VMEM((spots, block), f32),
+            pltpu.VMEM((spots, slots), f32),
             pltpu.VMEM((ITERS, mates, slots, block), f32),
             pltpu.VMEM((ITERS, slots, block), f32),
-            pltpu.VMEM((slots, block), f32),
+            pltpu.VMEM((spots, block), f32),
             pltpu.VMEM((ITERS, peers, stored_blocks, width), f32),
             pltpu.VMEM((ITERS, peers, stored_blocks, width), f32),
             pltpu.VMEM((ITERS, stored_blocks, width), f32),
@@ -339,6 +420,10 @@
             dma((ITERS,)),
             dma,
             dma,
+            dma,
+            dma,
+            dma((owners,)),
+            dma((owners,)),
         ],
         compiler_params=pltpu.CompilerParams(
             collective_id=0, has_side_effects=True, vmem_limit_bytes=50 * 2**20
@@ -346,13 +431,13 @@
         name="sweeps",
     )(
         male_features,
-        wanted,
+        female_features,
         male_mass.reshape(slots, block),
         female_mass.reshape(stored_blocks, block),
         base_interaction,
         reform_interaction,
-        pick,
-        live,
+        info,
+        spot_info,
     )
     return male_root.reshape(-1), female_root.reshape(-1)
 

time: 130 us -> 75.4 us (0.58)
  waiting for transfers between devices: 47.8 us -> 0 us
  between operations: 14.1 us -> 0.68 us
  Pallas kernels: 62.2 us -> 68.1 us
    all_gather x1 -> x0, waiting for transfers between devices: 47.1 us -> none  [body(): gathered = lax.all_gather(female_features, 'blk')]
    pallas_call x1, Pallas kernels: 56.8 us -> 68.1 us  [body(): pl.pallas_call(functools.partial(sweeps, (owners, n_sub, n_rep)), out_sha...]
    pallas_call x1 -> x0, Pallas kernels: 5.39 us -> none  [body(): pl.pallas_call(copy_block, grid_spec=pltpu.PrefetchScalarGridSpec(num_sca...]
    unnamed x10 -> x12, local copies, waits for them, and re-layouts: 1.05 us -> 3.55 us
  transfers between devices with their start and end apart: 1 -> 0, of which waited for: 1 -> 0; matrix products, arithmetic and copies ran while one was open for 2% -> 0% of each run, Pallas kernels for 0% -> 0%
where the time goes in v2:
time: 75.4 us; the launch traced here: 75 us
  Pallas kernels  68.1 us (90%)
  local copies, waits for them, and re-layouts  4.35 us (6%)
  other arithmetic  1.92 us (3%)
    pallas_call x1, Pallas kernels, body(): pl.pallas_call(functools.partial(sweeps, (owners, n_sub, n_rep)), out_sha...  68.1 us
    unnamed x12, local copies, waits for them, and re-layouts  3.55 us

profile of v2, /device:TPU:0, one launch (start us, length us, event | category | flops | bytes accessed | tf_op | source)
XLA Modules:
  0.0 75.0 jit_solution(14026279566455503886)
XLA Ops:
  0.6 0.0 copy-start.4
  0.6 0.9 %select_reduce_fusion.1 = s32[8]{0:T(128)S(1)} fusion(s32[32]{0:T(128)} %param.15, s32[8]{0:T(128)} %param.16), kind=kLoop, calls=%fused_computation.6 | loop fusion | flops 760 | bytes 192 | tf_op jit(solution)/shard_map/reduce_sum | solution.py:365
  1.5 0.2 convert_reduce_fusion
  1.7 0.7 pad_add_fusion
  2.4 0.1 iota_compare_fusion
  2.5 0.1 select_reduce_fusion
  2.6 0.1 broadcast_in_dim.38.info_ref
  2.6 0.1 broadcast_in_dim.60.spot_ref
  2.7 0.0 copy-done.4
  2.7 0.0 copy-start.5
  2.7 0.7 copy-done.5
  3.5 0.0 copy-start.2
  3.5 0.0 copy-start.3
  3.5 0.7 copy-done.2
  4.2 0.0 copy-done.3
  4.2 0.0 copy-start
  4.2 1.0 %copy-done = bf16[32,8192]{1,0:T(8,128)(2,1)S(1)} copy-done((bf16[32,8192]{1,0:T(8,128)(2,1)S(1)}, bf16[32,8192]{1,0:T(8,128)(2,1)}, u32[]{:S(2)}) %copy-start) | copy-done | bytes 524312
  5.3 0.0 copy-start.1
  5.3 1.0 %copy-done.1 = bf16[32,8192]{1,0:T(8,128)(2,1)S(1)} copy-done((bf16[32,8192]{1,0:T(8,128)(2,1)S(1)}, bf16[32,8192]{1,0:T(8,128)(2,1)}, u32[]{:S(2)}) %copy-start.1) | copy-done | bytes 524312
  6.3 68.1 %sweeps.1 = (f32[8,1024]{1,0:T(8,128)S(1)}, f32[8,1024]{1,0:T(8,128)S(1)}) custom-call(bf16[32,8192]{1,0:T(8,128)(2,1)S(1)} %copy-done, bf16[32,8192]{1,0:T(8,128)(2,1)S(1)} %copy-done.1, f32[8,1024]{1,0:T(8,128)S(1)} %reshape.157.mmass_ref, f32[8,1024]{1,0:T(8,128)S(1)} %reshape.158.fmass_ref, f32[32,32]{1,0:T(8,128)S(1)} %copy-done.2, ...), custom_call_target="tpu_custom_call" | custom-call | tf_op jit(solution)/shard_map/sweeps/pallas_call | solution.py:383
  74.4 0.6 copy_bitcast_fusion
  (7 shorter events, 0.1 us)
Async XLA Ops:
  0.6 2.1 %copy-start.4 = (f32[8192]{0:T(1024)S(1)}, f32[8192]{0:T(1024)}, u32[]{:S(2)}) copy-start(f32[8192]{0:T(1024)} %param.11) | copy-start | bytes 98308
  2.7 0.8 %copy-start.5 = (f32[8192]{0:T(1024)S(1)}, f32[8192]{0:T(1024)}, u32[]{:S(2)}) copy-start(f32[8192]{0:T(1024)} %param.12) | copy-start | bytes 98308
  3.5 0.7 copy-start.2
  3.5 0.7 copy-start.3
  4.2 1.0 %copy-start = (bf16[32,8192]{1,0:T(8,128)(2,1)S(1)}, bf16[32,8192]{1,0:T(8,128)(2,1)}, u32[]{:S(2)}) copy-start(bf16[32,8192]{1,0:T(8,128)(2,1)} %male_ref.1) | copy-start | bytes 1572868
  5.3 1.0 %copy-start.1 = (bf16[32,8192]{1,0:T(8,128)(2,1)S(1)}, bf16[32,8192]{1,0:T(8,128)(2,1)}, u32[]{:S(2)}) copy-start(bf16[32,8192]{1,0:T(8,128)(2,1)} %fem_ref.1) | copy-start | bytes 1572868

commit v3 on v2

--- a/solution.py
+++ b/solution.py
@@ -63,6 +63,8 @@
     ask_recv,
     fem_send,
     fem_recv,
+    men_sem,
+    women_sem,
 ):
     owners, n_sub, n_rep = sizes
     mates = n_sub * n_rep
@@ -72,56 +74,87 @@
     feat = male_ref.shape[0]
     spots = kern.shape[0]
     depth = spots // owners
-    width = col_out.shape[-1]
+    width = last_out.shape[-1]
     chunks = block // width
     group = lax.axis_index("groups")
     my_blk = lax.axis_index("blk")
     my_mate = lax.axis_index("sub") * n_rep + lax.axis_index("rep")
-    me = my_blk * mates + my_mate
-
-    def device_of(peer):
-        blk = lax.div(peer, mates)
-        mate = lax.rem(peer, mates)
-        return (group, blk, lax.div(mate, n_rep), lax.rem(mate, n_rep))
-
-    def mate_place(mate):
-        return (group, my_blk, lax.div(mate, n_rep), lax.rem(mate, n_rep))
+
+    my_sub = lax.axis_index("sub")
+    my_rep = lax.axis_index("rep")
+    sub_at = [lax.rem(my_sub + shift, n_sub) for shift in range(n_sub)]
+    rep_at = [lax.rem(my_rep + shift, n_rep) for shift in range(n_rep)]
+    around = [(sub, rep) for sub in range(n_sub) for rep in range(n_rep)]
+
+    def each_blk(act):
+        if owners <= 4:
+            for step in range(1, owners):
+                act(step)
+        else:
+            pl.loop(1, owners)(act)
+
+    def blk_at(step):
+        return lax.rem(my_blk + step, owners)
+
+    def slot_from(blk, mate):
+        step = lax.rem(my_blk - blk + owners, owners)
+        sub = lax.rem(my_sub - mate // n_rep + n_sub, n_sub)
+        return step * mates + sub * n_rep + lax.rem(my_rep - mate % n_rep + n_rep, n_rep)
 
     def wait_all(ref, sem):
         pltpu.make_async_copy(ref, ref, sem).wait()
 
+    for index in range(slots):
+        pltpu.make_async_copy(
+            male_ref.at[:, pl.ds(index * block, block)],
+            men.at[pl.ds(index * feat, feat)],
+            men_sem,
+        ).start()
+    for index in range(stored_blocks):
+        pltpu.make_async_copy(
+            fem_ref.at[:, pl.ds(index * block, block)],
+            women.at[pl.ds(index * feat, feat)],
+            women_sem,
+        ).start()
+
     barrier = pltpu.get_barrier_semaphore()
 
-    @pl.loop(1, peers)
-    def _(step):
-        pl.semaphore_signal(
-            barrier, inc=1, device_id=device_of(lax.rem(me + step, peers)), device_id_type=MESH
-        )
-
+    def greet(step, skip=False):
+        for sub, rep in around[1:] if skip else around:
+            pl.semaphore_signal(
+                barrier,
+                inc=1,
+                device_id=(group, blk_at(step), sub_at[sub], rep_at[rep]),
+                device_id_type=MESH,
+            )
+
+    greet(0, True)
+    each_blk(greet)
     pl.semaphore_wait(barrier, peers - 1)
 
     def to_peers(src_of, dst, send_sem, recv_sem):
-        @pl.loop(1, peers)
-        def _(step):
-            peer = lax.rem(me + step, peers)
+        def send(step, skip=False):
+            for sub, rep in around[1:] if skip else around:
+                pltpu.make_async_remote_copy(
+                    src_ref=src_of(step, sub_at[sub] * n_rep + rep_at[rep]),
+                    dst_ref=dst.at[step * mates + sub * n_rep + rep],
+                    send_sem=send_sem,
+                    recv_sem=recv_sem,
+                    device_id=(group, blk_at(step), sub_at[sub], rep_at[rep]),
+                    device_id_type=MESH,
+                ).start()
+
+        each_blk(send)
+        send(0, True)
+
+    def to_mates(src, dst, send_sem, recv_sem):
+        for sub, rep in around[1:]:
             pltpu.make_async_remote_copy(
-                src_ref=src_of(peer),
-                dst_ref=dst.at[step],
+                src_ref=src,
+                dst_ref=dst.at[sub * n_rep + rep],
                 send_sem=send_sem,
                 recv_sem=recv_sem,
-                device_id=device_of(peer),
-                device_id_type=MESH,
-            ).start()
-
-    def to_mates(src, dst, send_sem, recv_sem):
-        @pl.loop(1, mates)
-        def _(step):
-            pltpu.make_async_remote_copy(
-                src_ref=src,
-                dst_ref=dst.at[step],
-                send_sem=send_sem,
-                recv_sem=recv_sem,
-                device_id=mate_place(lax.rem(my_mate + step, mates)),
+                device_id=(group, my_blk, sub_at[sub], rep_at[rep]),
                 device_id_type=MESH,
             ).start()
 
@@ -129,14 +162,30 @@
         start = pl.multiple_of(lax.rem(my_mate, chunks) * width, width)
         return ref[:, pl.ds(start, width)]
 
+    def pack(piece):
+        parts = [piece[:, begin : begin + 128] for begin in range(0, width, 128)]
+        if len(parts) == 1:
+            parts = parts * 2
+        return jnp.concatenate(parts, axis=0).astype(jnp.bfloat16)
+
+    def unpack(packed):
+        tall = packed.astype(jnp.float32)
+        return jnp.concatenate(
+            [
+                tall[index * stored_blocks : (index + 1) * stored_blocks]
+                for index in range(width // 128)
+            ],
+            axis=1,
+        )
+
     def select_vals(turn):
         for owner in range(owners):
             for chunk in range(chunks):
-                index = lax.rem(me - (owner * mates + chunk) + peers, peers)
+                index = slot_from(owner, chunk)
                 vals[
                     owner * stored_blocks : (owner + 1) * stored_blocks,
                     chunk * width : (chunk + 1) * width,
-                ] = vals_in[turn, index]
+                ] = unpack(vals_in[turn, index])
         picked = jnp.dot(
             pick[...].astype(jnp.bfloat16),
             vals[...].astype(jnp.bfloat16),
@@ -151,10 +200,10 @@
         return jnp.broadcast_to(lines[pl.ds(slot, 1), :], (16, block)).astype(jnp.bfloat16)
 
     fmass_mine = my_chunk(fmass_ref)
-    first = jnp.sqrt(fmass_mine)
+    first = pack(jnp.sqrt(fmass_mine))
     vals_out[0] = first
     vals_in[0, 0] = first
-    to_peers(lambda peer: vals_out.at[0], vals_in.at[0], val_send.at[0], val_recv.at[0])
+    to_peers(lambda step, mate: vals_out.at[0], vals_in.at[0], val_send.at[0], val_recv.at[0])
     def mix(weights, lines_in):
         total = weights[:, :1] * lines_in[:1, :]
         for index in range(1, lines_in.shape[0]):
@@ -172,22 +221,18 @@
     for step in range(owners):
         ask_out[step, :depth] = local_at[step * depth : (step + 1) * depth]
 
-    @pl.loop(1, owners)
-    def _(step):
-        to = lax.rem(my_blk - step + owners, owners) * mates + my_mate
+    def ask(step):
         pltpu.make_async_remote_copy(
             src_ref=ask_out.at[step],
             dst_ref=ask_in.at[step],
             send_sem=ask_send,
             recv_sem=ask_recv,
-            device_id=device_of(to),
+            device_id=(group, blk_at(owners - step), my_sub, my_rep),
             device_id_type=MESH,
         ).start()
 
-    for index in range(slots):
-        men[index * feat : (index + 1) * feat] = male_ref[:, index * block : (index + 1) * block]
-    for index in range(stored_blocks):
-        women[index * feat : (index + 1) * feat] = fem_ref[:, index * block : (index + 1) * block]
+    each_blk(ask)
+    wait_all(women, women_sem)
 
     def choose(line, source):
         total = source.shape[0]
@@ -201,21 +246,22 @@
         fem_in[deep] = choose(ask_out[0, deep : deep + 1], women).astype(jnp.bfloat16)
     wait_all(ask_in.at[pl.ds(1, owners - 1)], ask_recv)
 
-    @pl.loop(1, owners)
-    def _(step):
+    def reply(step):
         for deep in range(depth):
             fem_out[step * depth + deep] = choose(
                 ask_in[step, deep : deep + 1], women
             ).astype(jnp.bfloat16)
-        to = lax.rem(my_blk + step, owners) * mates + my_mate
         pltpu.make_async_remote_copy(
             src_ref=fem_out.at[pl.ds(step * depth, depth)],
             dst_ref=fem_in.at[pl.ds(step * depth, depth)],
             send_sem=fem_send.at[step],
             recv_sem=fem_recv.at[step],
-            device_id=device_of(to),
+            device_id=(group, blk_at(step), my_sub, my_rep),
             device_id_type=MESH,
         ).start()
+
+    each_blk(reply)
+    wait_all(men, men_sem)
 
     wait_all(vals_in.at[0, pl.ds(1, peers - 1)], val_recv.at[0])
     select_vals(0)
@@ -272,9 +318,9 @@
         row_in[sweep, 0] = partial
         to_mates(row_out.at[sweep], row_in.at[sweep], row_send.at[sweep], row_recv.at[sweep])
         wait_all(row_in.at[sweep, pl.ds(1, mates - 1)], row_recv.at[sweep])
-        totals = row_in[sweep, lax.rem(my_mate + mates, mates)]
+        totals = row_in[sweep, slot_from(my_blk, 0)]
         for mate in range(1, mates):
-            totals = totals + row_in[sweep, lax.rem(my_mate - mate + mates, mates)]
+            totals = totals + row_in[sweep, slot_from(my_blk, mate)]
         male_pot = solve_pot(totals, mmass_ref[...])
         lines[...] = mix(place_t[...], male_pot)
         if sweep == ITERS - 1:
@@ -285,38 +331,45 @@
             total = jnp.dot(line_of(slot), kern[slot], preferred_element_type=jnp.float32)
             cols[pl.ds(slot, 1), :] = total[0:1]
 
-        dense = lax.dot_general(
-            pick[...],
-            jnp.where(live_at[:, :1] > 0.0, cols[...], 0.0),
-            (((0,), (0,)), ((), ())),
-            precision=lax.Precision.HIGHEST,
-            preferred_element_type=jnp.float32,
-        )
-        for owner in range(owners):
-            for mate in range(mates):
-                begin = (mate % chunks) * width
-                col_out[sweep, owner * mates + mate] = dense[
-                    owner * stored_blocks : (owner + 1) * stored_blocks, begin : begin + width
-                ]
-
-        col_in[sweep, 0] = col_out[sweep, me]
+        columns = jnp.where(live_at[:, :1] > 0.0, cols[...], 0.0)
+        for chunk in range(chunks):
+            for step in range(owners):
+                span = slice(step * depth, (step + 1) * depth)
+                col_out[sweep, chunk, step] = jnp.concatenate(
+                    [columns[span, chunk * width : (chunk + 1) * width], local_at[span]], axis=1
+                )
+
+        col_in[sweep, 0] = col_out[sweep, lax.rem(my_mate, chunks), 0]
         to_peers(
-            lambda peer: col_out.at[sweep, peer],
+            lambda step, mate: col_out.at[
+                sweep, lax.rem(mate, chunks), lax.rem(owners - step, owners)
+            ],
             col_in.at[sweep],
             col_send.at[sweep],
             col_recv.at[sweep],
         )
         wait_all(col_in.at[sweep, pl.ds(1, peers - 1)], col_recv.at[sweep])
+        blocks_row = lax.broadcasted_iota(jnp.int32, (stored_blocks, 128), 0).astype(jnp.float32)
+
+        def gather_piece(step, total):
+            piece = col_in[sweep, step]
+            for deep in range(depth):
+                here = jnp.where(blocks_row == piece[deep : deep + 1, width:], 1.0, 0.0)
+                here = jnp.concatenate([here] * (width // 128), axis=1)
+                total = total + here * piece[deep : deep + 1, :width]
+            return total
+
         col_total = lax.fori_loop(
-            1, peers, lambda step, total: total + col_in[sweep, step], col_in[sweep, 0]
+            0, peers, gather_piece, jnp.zeros((stored_blocks, width), jnp.float32)
         )
         female_pot = solve_pot(col_total, fmass_mine)
         if sweep < ITERS - 1:
             turn = sweep + 1
-            vals_out[turn] = female_pot
-            vals_in[turn, 0] = female_pot
+            packed = pack(female_pot)
+            vals_out[turn] = packed
+            vals_in[turn, 0] = packed
             to_peers(
-                lambda peer: vals_out.at[turn], vals_in.at[turn], val_send.at[turn], val_recv.at[turn]
+                lambda step, mate: vals_out.at[turn], vals_in.at[turn], val_send.at[turn], val_recv.at[turn]
             )
             wait_all(vals_in.at[turn, pl.ds(1, peers - 1)], val_recv.at[turn])
             select_vals(turn)
@@ -328,7 +381,7 @@
             wait_all(last_in.at[pl.ds(1, mates - 1)], last_recv)
             for chunk in range(chunks):
                 froot_ref[:, chunk * width : (chunk + 1) * width] = last_in[
-                    lax.rem(my_mate - chunk + mates, mates)
+                    slot_from(my_blk, chunk)
                 ]
 
     for sweep in range(ITERS):
@@ -378,6 +431,7 @@
     spot_info = jnp.broadcast_to(spot_info.astype(jnp.float32)[:, :, None], (4, spots, 128))
     feat = male_features.shape[0]
     vmem = pl.BlockSpec(memory_space=pltpu.VMEM)
+    anywhere = pl.BlockSpec(memory_space=pl.ANY)
     dma = pltpu.SemaphoreType.DMA
     f32 = jnp.float32
     male_root, female_root = pl.pallas_call(
@@ -386,7 +440,7 @@
             jax.ShapeDtypeStruct((slots, block), f32),
             jax.ShapeDtypeStruct((stored_blocks, block), f32),
         ),
-        in_specs=[vmem] * 8,
+        in_specs=[anywhere] * 2 + [vmem] * 6,
         out_specs=(vmem, vmem),
         scratch_shapes=[
             pltpu.VMEM((spots, block, block), jnp.bfloat16),
@@ -406,10 +460,10 @@
             pltpu.VMEM((ITERS, mates, slots, block), f32),
             pltpu.VMEM((ITERS, slots, block), f32),
             pltpu.VMEM((spots, block), f32),
-            pltpu.VMEM((ITERS, peers, stored_blocks, width), f32),
-            pltpu.VMEM((ITERS, peers, stored_blocks, width), f32),
-            pltpu.VMEM((ITERS, stored_blocks, width), f32),
-            pltpu.VMEM((ITERS, peers, stored_blocks, width), f32),
+            pltpu.VMEM((ITERS, block // width, owners, spot_depth, width + 128), f32),
+            pltpu.VMEM((ITERS, peers, spot_depth, width + 128), f32),
+            pltpu.VMEM((ITERS, max(16, stored_blocks * width // 128), 128), jnp.bfloat16),
+            pltpu.VMEM((ITERS, peers, max(16, stored_blocks * width // 128), 128), jnp.bfloat16),
             pltpu.VMEM((stored_blocks, width), f32),
             pltpu.VMEM((mates, stored_blocks, width), f32),
             dma((ITERS,)),
@@ -424,6 +478,8 @@
             dma,
             dma((owners,)),
             dma((owners,)),
+            dma,
+            dma,
         ],
         compiler_params=pltpu.CompilerParams(
             collective_id=0, has_side_effects=True, vmem_limit_bytes=50 * 2**20

time: 75.4 us -> 72 us (0.955)
  Pallas kernels: 68.1 us -> 64.7 us
    pallas_call x1, Pallas kernels: 68.1 us -> 64.7 us  [body(): pl.pallas_call(functools.partial(sweeps, (owners, n_sub, n_rep)), out_sha...]
where the time goes in v3:
time: 72 us; the launch traced here: 71.6 us
  Pallas kernels  64.7 us (90%)
  local copies, waits for them, and re-layouts  4.35 us (6%)
  other arithmetic  1.92 us (3%)
    pallas_call x1, Pallas kernels, body(): pl.pallas_call(functools.partial(sweeps, (owners, n_sub, n_rep)), out_sha...  64.7 us
    unnamed x12, local copies, waits for them, and re-layouts  3.55 us

profile of v3, /device:TPU:0, one launch (start us, length us, event | category | flops | bytes accessed | tf_op | source)
XLA Modules:
  0.0 71.6 jit_solution(2972951622191024878)
XLA Ops:
  0.6 0.0 copy-start.4
  0.6 0.9 %select_reduce_fusion.1 = s32[8]{0:T(128)S(1)} fusion(s32[32]{0:T(128)} %param.15, s32[8]{0:T(128)} %param.16), kind=kLoop, calls=%fused_computation.6 | loop fusion | flops 760 | bytes 192 | tf_op jit(solution)/shard_map/reduce_sum | solution.py:418
  1.5 0.2 convert_reduce_fusion
  1.7 0.7 pad_add_fusion
  2.4 0.1 iota_compare_fusion
  2.5 0.1 select_reduce_fusion
  2.6 0.1 broadcast_in_dim.38.info_ref
  2.6 0.1 broadcast_in_dim.60.spot_ref
  2.7 0.0 copy-done.4
  2.7 0.0 copy-start.5
  2.7 0.7 %copy-done.5 = f32[8192]{0:T(1024)S(1)} copy-done((f32[8192]{0:T(1024)S(1)}, f32[8192]{0:T(1024)}, u32[]{:S(2)}) %copy-start.5) | copy-done | bytes 32792
  3.5 0.0 copy-start.2
  3.5 0.0 copy-start.3
  3.5 0.7 copy-done.2
  4.2 0.0 copy-done.3
  4.2 0.0 copy-start
  4.2 1.0 %copy-done = bf16[32,8192]{1,0:T(8,128)(2,1)S(1)} copy-done((bf16[32,8192]{1,0:T(8,128)(2,1)S(1)}, bf16[32,8192]{1,0:T(8,128)(2,1)}, u32[]{:S(2)}) %copy-start) | copy-done | bytes 524312
  5.3 0.0 copy-start.1
  5.3 1.0 %copy-done.1 = bf16[32,8192]{1,0:T(8,128)(2,1)S(1)} copy-done((bf16[32,8192]{1,0:T(8,128)(2,1)S(1)}, bf16[32,8192]{1,0:T(8,128)(2,1)}, u32[]{:S(2)}) %copy-start.1) | copy-done | bytes 524312
  6.3 64.7 %sweeps.1 = (f32[8,1024]{1,0:T(8,128)S(1)}, f32[8,1024]{1,0:T(8,128)S(1)}) custom-call(bf16[32,8192]{1,0:T(8,128)(2,1)S(1)} %copy-done, bf16[32,8192]{1,0:T(8,128)(2,1)S(1)} %copy-done.1, f32[8,1024]{1,0:T(8,128)S(1)} %reshape.157.mmass_ref, f32[8,1024]{1,0:T(8,128)S(1)} %reshape.158.fmass_ref, f32[32,32]{1,0:T(8,128)S(1)} %copy-done.2, ...), custom_call_target="tpu_custom_call" | custom-call | tf_op jit(solution)/shard_map/sweeps/pallas_call | solution.py:437
  71.0 0.6 copy_bitcast_fusion
  (7 shorter events, 0.1 us)
Async XLA Ops:
  0.6 2.1 %copy-start.4 = (f32[8192]{0:T(1024)S(1)}, f32[8192]{0:T(1024)}, u32[]{:S(2)}) copy-start(f32[8192]{0:T(1024)} %param.11) | copy-start | bytes 98308
  2.7 0.8 %copy-start.5 = (f32[8192]{0:T(1024)S(1)}, f32[8192]{0:T(1024)}, u32[]{:S(2)}) copy-start(f32[8192]{0:T(1024)} %param.12) | copy-start | bytes 98308
  3.5 0.7 %copy-start.2 = (f32[32,32]{1,0:T(8,128)S(1)}, f32[32,32]{1,0:T(8,128)}, u32[]{:S(2)}) copy-start(f32[32,32]{1,0:T(8,128)} %base_ref.1) | copy-start | bytes 12292
  3.5 0.7 %copy-start.3 = (f32[32,32]{1,0:T(8,128)S(1)}, f32[32,32]{1,0:T(8,128)}, u32[]{:S(2)}) copy-start(f32[32,32]{1,0:T(8,128)} %reform_ref.1) | copy-start | bytes 12292
  4.2 1.0 %copy-start = (bf16[32,8192]{1,0:T(8,128)(2,1)S(1)}, bf16[32,8192]{1,0:T(8,128)(2,1)}, u32[]{:S(2)}) copy-start(bf16[32,8192]{1,0:T(8,128)(2,1)} %male_ref.1) | copy-start | bytes 1572868
  5.3 1.0 %copy-start.1 = (bf16[32,8192]{1,0:T(8,128)(2,1)S(1)}, bf16[32,8192]{1,0:T(8,128)(2,1)}, u32[]{:S(2)}) copy-start(bf16[32,8192]{1,0:T(8,128)(2,1)} %fem_ref.1) | copy-start | bytes 1572868

commit v4 on v3

--- a/solution.py
+++ b/solution.py
@@ -196,9 +196,7 @@
         )
         line_t[...] = padded.T.astype(jnp.bfloat16)
 
-    def line_of(slot):
-        return jnp.broadcast_to(lines[pl.ds(slot, 1), :], (16, block)).astype(jnp.bfloat16)
-
+    middle_row = block // 2
     fmass_mine = my_chunk(fmass_ref)
     first = pack(jnp.sqrt(fmass_mine))
     vals_out[0] = first
@@ -273,10 +271,9 @@
     for sweep in range(ITERS):
 
         row_t[...] = jnp.zeros_like(row_t)
-
-        @pl.loop(0, spots)
-        def _(spot):
-            height = block // 4
+        height = block // 4
+
+        def row_pass(spot, parts):
             if sweep == 0:
 
                 @pl.when(jnp.logical_and(spot >= depth, lax.rem(spot, depth) == 0))
@@ -302,7 +299,7 @@
                 right = jnp.concatenate(
                     [fem, fem, fem, jnp.ones((16, block), jnp.bfloat16)], axis=0
                 )
-            for part in range(4):
+            for part in parts:
                 span = slice(part * height, (part + 1) * height)
                 if sweep == 0:
                     scores = jnp.dot(left[span], right, preferred_element_type=jnp.float32)
@@ -313,23 +310,51 @@
                 total = jnp.dot(tile, line_t[...], preferred_element_type=jnp.float32)
                 row_t[span, :] = row_t[span, :] + jnp.where(column == spot, total, 0.0)
 
-        partial = mix(place[...], jnp.where(live_at[:, :1] > 0.0, row_t[...].T[:spots], 0.0))
-        row_out[sweep] = partial
-        row_in[sweep, 0] = partial
-        to_mates(row_out.at[sweep], row_in.at[sweep], row_send.at[sweep], row_recv.at[sweep])
-        wait_all(row_in.at[sweep, pl.ds(1, mates - 1)], row_recv.at[sweep])
-        totals = row_in[sweep, slot_from(my_blk, 0)]
-        for mate in range(1, mates):
-            totals = totals + row_in[sweep, slot_from(my_blk, mate)]
-        male_pot = solve_pot(totals, mmass_ref[...])
-        lines[...] = mix(place_t[...], male_pot)
-        if sweep == ITERS - 1:
-            mroot_ref[...] = male_pot / jnp.sqrt(mmass_ref[...])
-
-        @pl.loop(0, spots)
-        def _(slot):
-            total = jnp.dot(line_of(slot), kern[slot], preferred_element_type=jnp.float32)
-            cols[pl.ds(slot, 1), :] = total[0:1]
+        def send_rows(half):
+            tall = row_t[half * middle_row : (half + 1) * middle_row, :].T[:spots]
+            partial = mix(place[...], jnp.where(live_at[:, :1] > 0.0, tall, 0.0))
+            row_out[sweep, half] = partial
+            row_in[sweep, half, 0] = partial
+            to_mates(
+                row_out.at[sweep, half],
+                row_in.at[sweep, half],
+                row_send.at[sweep, half],
+                row_recv.at[sweep, half],
+            )
+
+        if sweep == 0:
+            pl.loop(0, spots)(lambda spot: row_pass(spot, range(4)))
+            send_rows(0)
+            send_rows(1)
+        else:
+            for half in range(2):
+                pl.loop(0, spots)(lambda spot: row_pass(spot, range(2 * half, 2 * half + 2)))
+                send_rows(half)
+
+        for half in range(2):
+            span = slice(half * middle_row, (half + 1) * middle_row)
+            wait_all(row_in.at[sweep, half, pl.ds(1, mates - 1)], row_recv.at[sweep, half])
+            totals = row_in[sweep, half, slot_from(my_blk, 0)]
+            for mate in range(1, mates):
+                totals = totals + row_in[sweep, half, slot_from(my_blk, mate)]
+            mass = mmass_ref[:, span]
+            male_pot = solve_pot(totals, mass)
+            lines[:, span] = mix(place_t[...], male_pot)
+            if sweep == ITERS - 1:
+                mroot_ref[:, span] = male_pot / jnp.sqrt(mass)
+
+            @pl.loop(0, spots)
+            def _(spot):
+                line = jnp.broadcast_to(lines[pl.ds(spot, 1), span], (16, middle_row))
+                total = jnp.dot(
+                    line.astype(jnp.bfloat16),
+                    kern[spot, span, :],
+                    preferred_element_type=jnp.float32,
+                )[0:1]
+                if half == 0:
+                    cols[pl.ds(spot, 1), :] = total
+                else:
+                    cols[pl.ds(spot, 1), :] = cols[pl.ds(spot, 1), :] + total
 
         columns = jnp.where(live_at[:, :1] > 0.0, cols[...], 0.0)
         for chunk in range(chunks):
@@ -385,7 +410,8 @@
                 ]
 
     for sweep in range(ITERS):
-        wait_all(row_in.at[sweep, pl.ds(1, mates - 1)], row_send.at[sweep])
+        for half in range(2):
+            wait_all(row_in.at[sweep, half, pl.ds(1, mates - 1)], row_send.at[sweep, half])
         wait_all(col_in.at[sweep, pl.ds(1, peers - 1)], col_send.at[sweep])
         wait_all(vals_in.at[sweep, pl.ds(1, peers - 1)], val_send.at[sweep])
     wait_all(last_in.at[pl.ds(1, mates - 1)], last_send)
@@ -457,8 +483,8 @@
             pltpu.VMEM((owners * stored_blocks, block), f32),
             pltpu.VMEM((spots, block), f32),
             pltpu.VMEM((spots, slots), f32),
-            pltpu.VMEM((ITERS, mates, slots, block), f32),
-            pltpu.VMEM((ITERS, slots, block), f32),
+            pltpu.VMEM((ITERS, 2, mates, slots, block // 2), f32),
+            pltpu.VMEM((ITERS, 2, slots, block // 2), f32),
             pltpu.VMEM((spots, block), f32),
             pltpu.VMEM((ITERS, block // width, owners, spot_depth, width + 128), f32),
             pltpu.VMEM((ITERS, peers, spot_depth, width + 128), f32),
@@ -466,8 +492,8 @@
             pltpu.VMEM((ITERS, peers, max(16, stored_blocks * width // 128), 128), jnp.bfloat16),
             pltpu.VMEM((stored_blocks, width), f32),
             pltpu.VMEM((mates, stored_blocks, width), f32),
-            dma((ITERS,)),
-            dma((ITERS,)),
+            dma((ITERS, 2)),
+            dma((ITERS, 2)),
             dma((ITERS,)),
             dma((ITERS,)),
             dma((ITERS,)),
@@ -482,7 +508,7 @@
             dma,
         ],
         compiler_params=pltpu.CompilerParams(
-            collective_id=0, has_side_effects=True, vmem_limit_bytes=50 * 2**20
+            collective_id=0, has_side_effects=True, vmem_limit_bytes=60 * 2**20
         ),
         name="sweeps",
     )(

time: 72 us -> 73.7 us (1.024)
  Pallas kernels: 64.7 us -> 66.5 us
    unnamed x12 -> x4, local copies, waits for them, and re-layouts: 3.55 us -> 0.13 us
    pallas_call x1, Pallas kernels: 64.7 us -> 66.5 us  [body(): pl.pallas_call(functools.partial(sweeps, (owners, n_sub, n_rep)), out_sha...]
    reshape x1, local copies, waits for them, and re-layouts: 0.63 us -> 1.41 us  [body(): return (male_root.reshape(-1), female_root.reshape(-1))]
where the time goes in v4:
time: 73.7 us; the launch traced here: 73.2 us
  Pallas kernels  66.5 us (90%)
  local copies, waits for them, and re-layouts  4.13 us (6%)
  other arithmetic  1.92 us (3%)
    pallas_call x1, Pallas kernels, body(): pl.pallas_call(functools.partial(sweeps, (owners, n_sub, n_rep)), out_sha...  66.5 us

profile of v4, /device:TPU:0, one launch (start us, length us, event | category | flops | bytes accessed | tf_op | source)
XLA Modules:
  0.0 73.2 jit_solution(13987562115666432829)
XLA Ops:
  0.6 0.0 copy-start
  0.6 0.9 %select_reduce_fusion.1 = s32[8]{0:T(128)S(1)} fusion(s32[32]{0:T(128)} %param.15, s32[8]{0:T(128)} %param.16), kind=kLoop, calls=%fused_computation.6 | loop fusion | flops 760 | bytes 192 | tf_op jit(solution)/shard_map/reduce_sum | solution.py:444
  1.5 0.2 convert_reduce_fusion
  1.7 0.7 pad_add_fusion
  2.4 0.1 iota_compare_fusion
  2.5 0.1 select_reduce_fusion
  2.6 0.7 broadcast_in_dim.38.info_ref
  3.2 0.7 broadcast_in_dim.60.spot_ref
  3.9 0.0 copy-done
  3.9 0.0 copy-start.1
  3.9 0.6 reshape.157.mmass_ref
  4.5 0.1 copy-done.1
  4.7 0.6 reshape.158.fmass_ref
  5.3 66.5 %sweeps.1 = (f32[8,1024]{1,0:T(8,128)}, f32[8,1024]{1,0:T(8,128)}) custom-call(bf16[32,8192]{1,0:T(8,128)(2,1)} %male_ref.1, bf16[32,8192]{1,0:T(8,128)(2,1)} %fem_ref.1, f32[8,1024]{1,0:T(8,128)} %reshape.157.mmass_ref, f32[8,1024]{1,0:T(8,128)} %reshape.158.fmass_ref, f32[32,32]{1,0:T(8,128)} %base_ref.1, f32[32,32]{1,0:T(8,128)} %reform_ref.1, ...), custom_call_target="tpu_custom_call" | custom-call | tf_op jit(solution)/shard_map/sweeps/pallas_call | solution.py:463
  71.8 1.4 %copy_bitcast_fusion = (f32[8192]{0:T(1024)}, f32[8192]{0:T(1024)}) fusion(f32[1,8,8,128]{3,2,1,0:T(8,128)} %bitcast.10, f32[1,8,8,128]{3,2,1,0:T(8,128)} %bitcast.9), kind=kLoop, calls=%fused_computation | loop fusion | bytes 131072 | tf_op jit(solution)/shard_map/reshape | solution.py:524
  (5 shorter events, 0.1 us)
Async XLA Ops:
  0.6 3.3 %copy-start = (f32[8192]{0:T(1024)S(1)}, f32[8192]{0:T(1024)}, u32[]{:S(2)}) copy-start(f32[8192]{0:T(1024)} %param.11) | copy-start | bytes 98308
  3.9 0.8 %copy-start.1 = (f32[8192]{0:T(1024)S(1)}, f32[8192]{0:T(1024)}, u32[]{:S(2)}) copy-start(f32[8192]{0:T(1024)} %param.12) | copy-start | bytes 98308

commit v5 on v3

--- a/solution.py
+++ b/solution.py
@@ -274,7 +274,7 @@
 
         row_t[...] = jnp.zeros_like(row_t)
 
-        @pl.loop(0, spots)
+        @pl.loop(0, spots, unroll=2 if sweep > 0 and spots % 2 == 0 else 1)
         def _(spot):
             height = block // 4
             if sweep == 0:
@@ -326,7 +326,7 @@
         if sweep == ITERS - 1:
             mroot_ref[...] = male_pot / jnp.sqrt(mmass_ref[...])
 
-        @pl.loop(0, spots)
+        @pl.loop(0, spots, unroll=2 if spots % 2 == 0 else 1)
         def _(slot):
             total = jnp.dot(line_of(slot), kern[slot], preferred_element_type=jnp.float32)
             cols[pl.ds(slot, 1), :] = total[0:1]

time: 72 us -> 70.5 us (0.979)
  Pallas kernels: 64.7 us -> 63.1 us
    pallas_call x1, Pallas kernels: 64.7 us -> 63.1 us  [body(): pl.pallas_call(functools.partial(sweeps, (owners, n_sub, n_rep)), out_sha...]
where the time goes in v5:
time: 70.5 us; the launch traced here: 70.1 us
  Pallas kernels  63.1 us (90%)
  local copies, waits for them, and re-layouts  4.35 us (6%)
  other arithmetic  1.92 us (3%)
    pallas_call x1, Pallas kernels, body(): pl.pallas_call(functools.partial(sweeps, (owners, n_sub, n_rep)), out_sha...  63.1 us
    unnamed x12, local copies, waits for them, and re-layouts  3.55 us

profile of v5, /device:TPU:0, one launch (start us, length us, event | category | flops | bytes accessed | tf_op | source)
XLA Modules:
  0.0 70.1 jit_solution(2394136166546749512)
XLA Ops:
  0.6 0.0 copy-start.4
  0.6 0.9 %select_reduce_fusion.1 = s32[8]{0:T(128)S(1)} fusion(s32[32]{0:T(128)} %param.15, s32[8]{0:T(128)} %param.16), kind=kLoop, calls=%fused_computation.6 | loop fusion | flops 760 | bytes 192 | tf_op jit(solution)/shard_map/reduce_sum | solution.py:418
  1.5 0.2 convert_reduce_fusion
  1.7 0.7 pad_add_fusion
  2.4 0.1 iota_compare_fusion
  2.5 0.1 select_reduce_fusion
  2.6 0.1 broadcast_in_dim.38.info_ref
  2.6 0.1 broadcast_in_dim.60.spot_ref
  2.7 0.0 copy-done.4
  2.7 0.0 copy-start.5
  2.7 0.7 %copy-done.5 = f32[8192]{0:T(1024)S(1)} copy-done((f32[8192]{0:T(1024)S(1)}, f32[8192]{0:T(1024)}, u32[]{:S(2)}) %copy-start.5) | copy-done | bytes 32792
  3.5 0.0 copy-start.2
  3.5 0.0 copy-start.3
  3.5 0.7 copy-done.2
  4.2 0.0 copy-done.3
  4.2 0.0 copy-start
  4.2 1.0 %copy-done = bf16[32,8192]{1,0:T(8,128)(2,1)S(1)} copy-done((bf16[32,8192]{1,0:T(8,128)(2,1)S(1)}, bf16[32,8192]{1,0:T(8,128)(2,1)}, u32[]{:S(2)}) %copy-start) | copy-done | bytes 524312
  5.3 0.0 copy-start.1
  5.3 1.0 %copy-done.1 = bf16[32,8192]{1,0:T(8,128)(2,1)S(1)} copy-done((bf16[32,8192]{1,0:T(8,128)(2,1)S(1)}, bf16[32,8192]{1,0:T(8,128)(2,1)}, u32[]{:S(2)}) %copy-start.1) | copy-done | bytes 524312
  6.3 63.1 %sweeps.1 = (f32[8,1024]{1,0:T(8,128)S(1)}, f32[8,1024]{1,0:T(8,128)S(1)}) custom-call(bf16[32,8192]{1,0:T(8,128)(2,1)S(1)} %copy-done, bf16[32,8192]{1,0:T(8,128)(2,1)S(1)} %copy-done.1, f32[8,1024]{1,0:T(8,128)S(1)} %reshape.157.mmass_ref, f32[8,1024]{1,0:T(8,128)S(1)} %reshape.158.fmass_ref, f32[32,32]{1,0:T(8,128)S(1)} %copy-done.2, ...), custom_call_target="tpu_custom_call" | custom-call | tf_op jit(solution)/shard_map/sweeps/pallas_call | solution.py:437
  69.4 0.6 copy_bitcast_fusion
  (7 shorter events, 0.1 us)
Async XLA Ops:
  0.6 2.1 %copy-start.4 = (f32[8192]{0:T(1024)S(1)}, f32[8192]{0:T(1024)}, u32[]{:S(2)}) copy-start(f32[8192]{0:T(1024)} %param.11) | copy-start | bytes 98308
  2.7 0.8 %copy-start.5 = (f32[8192]{0:T(1024)S(1)}, f32[8192]{0:T(1024)}, u32[]{:S(2)}) copy-start(f32[8192]{0:T(1024)} %param.12) | copy-start | bytes 98308
  3.5 0.7 %copy-start.2 = (f32[32,32]{1,0:T(8,128)S(1)}, f32[32,32]{1,0:T(8,128)}, u32[]{:S(2)}) copy-start(f32[32,32]{1,0:T(8,128)} %base_ref.1) | copy-start | bytes 12292
  3.5 0.7 %copy-start.3 = (f32[32,32]{1,0:T(8,128)S(1)}, f32[32,32]{1,0:T(8,128)}, u32[]{:S(2)}) copy-start(f32[32,32]{1,0:T(8,128)} %reform_ref.1) | copy-start | bytes 12292
  4.2 1.0 %copy-start = (bf16[32,8192]{1,0:T(8,128)(2,1)S(1)}, bf16[32,8192]{1,0:T(8,128)(2,1)}, u32[]{:S(2)}) copy-start(bf16[32,8192]{1,0:T(8,128)(2,1)} %male_ref.1) | copy-start | bytes 1572868
  5.3 1.0 %copy-start.1 = (bf16[32,8192]{1,0:T(8,128)(2,1)S(1)}, bf16[32,8192]{1,0:T(8,128)(2,1)}, u32[]{:S(2)}) copy-start(bf16[32,8192]{1,0:T(8,128)(2,1)} %fem_ref.1) | copy-start | bytes 1572868
